TPU v7x, 128 devices: a whole 4x4x4 slice. The times are simulated.
128 devices in a mesh: prefix: 8 (over z_lo, y), resp: 8 (over x, core), mp: 2 (over z_hi).
Axes of the slice: x: 4, y: 4, z: 4 (z_hi: 2, z_lo: 2; z = z_hi * 2 + z_lo), core: 2. Of those that a mesh axis runs over, the one named last changes fastest.
Arguments:
- queries: bfloat16 [16, 1024, 32, 128], P('prefix', ('resp', 'mp')), may hold values from -6 to 6
- resp_keys: bfloat16 [16, 1024, 4, 128], P('prefix', ('resp', 'mp')), may hold values from -6 to 6
- resp_values: bfloat16 [16, 1024, 4, 128], P('prefix', ('resp', 'mp')), may hold values from -6 to 6
- prefix_keys: bfloat16 [2, 2048, 4, 128], P(None, 'prefix', 'mp'), may hold values from -6 to 6
- prefix_values: bfloat16 [2, 2048, 4, 128], P(None, 'prefix', 'mp'), may hold values from -6 to 6
- grad_out: bfloat16 [16, 1024, 32, 128], P('prefix', ('resp', 'mp')), may hold values from -6 to 6
- prompt_ids: int32 [16], replicated, may hold values from 0 to 1
- prefix_lengths: int32 [2], replicated, may hold values from 512 to 2048, as said below
- resp_lengths: int32 [16], replicated, may hold values from 1 to 1024, 10240 in all
Outputs:
- attention: bfloat16 [16, 1024, 32, 128], P('prefix', ('resp', 'mp'))
- d_queries: bfloat16 [16, 1024, 32, 128], P('prefix', ('resp', 'mp'))
- d_resp_keys: bfloat16 [16, 1024, 4, 128], P('prefix', ('resp', 'mp'))
- d_resp_values: bfloat16 [16, 1024, 4, 128], P('prefix', ('resp', 'mp'))
- d_prefix_keys: bfloat16 [2, 2048, 4, 128], P(None, 'prefix', 'mp')
- d_prefix_values: bfloat16 [2, 2048, 4, 128], P(None, 'prefix', 'mp')
Inputs may be any that keep to these rules, and one draw needn't show every extreme that they name: `prefix_lengths`: some prompt has all 2048 prefix positions valid. `resp_lengths`: some response has all 1024 positions valid.
All inputs are finite; a program needn't handle non-finite values.
Results may differ from a plain program's by a relative error of at most 0.04.
Values may be sent and summed in bfloat16 or wider, within the bound.
A program may use at most 192 MiB of HBM per device.

v0:
```python
import math

import jax
import jax.numpy as jnp
from jax import lax
from jax.sharding import PartitionSpec as P

NEG = -1e30


def block_scores(head_q, keys_block, key_start, positions, length, inv_root):
    key_count = keys_block.shape[0]
    raw_scores = (
        jnp.einsum("tgd,sd->tgs", head_q, keys_block, preferred_element_type=jnp.float32) * inv_root
    )
    key_pos = key_start + jnp.arange(key_count, dtype=jnp.int32)
    is_valid = (key_pos[None, :] <= positions[:, None]) & (key_pos[None, :] < length)
    return jnp.where(is_valid[:, None, :], raw_scores, NEG)


def head_pass(
    head_q, head_cot, keys_p, values_p, keys_r, values_r, prefix_len, length, positions, blocks
):
    shard_rows = head_q.shape[0]
    inv_root = 1.0 / math.sqrt(head_q.shape[-1])
    prefix_live = jnp.arange(keys_p.shape[0], dtype=jnp.int32) < prefix_len
    scores_p = (
        jnp.einsum("tgd,sd->tgs", head_q, keys_p, preferred_element_type=jnp.float32) * inv_root
    )
    scores_p = jnp.where(prefix_live[None, None, :], scores_p, NEG)
    row_max = jnp.max(scores_p, axis=-1)
    row_total = jnp.sum(jnp.exp(scores_p - row_max[..., None]), axis=-1)

    def resp_scores(block_index):
        key_start = block_index * shard_rows
        keys_block = lax.dynamic_slice_in_dim(keys_r, key_start, shard_rows, 0)
        return (block_scores(head_q, keys_block, key_start, positions, length, inv_root), key_start)

    def stat_step(block_index, state):
        old_max, old_total = state
        scores, key_start = resp_scores(block_index)
        new_max = jnp.maximum(old_max, jnp.max(scores, axis=-1))
        new_total = old_total * jnp.exp(old_max - new_max) + jnp.sum(
            jnp.exp(scores - new_max[..., None]), axis=-1
        )
        return (new_max, new_total)

    row_max, row_total = lax.fori_loop(0, blocks, stat_step, (row_max, row_total))
    log_total = row_max + jnp.log(row_total)
    probs_p = jnp.exp(scores_p - log_total[..., None])
    weights_p = probs_p.astype(jnp.bfloat16)
    attended = jnp.einsum("tgs,sd->tgd", weights_p, values_p, preferred_element_type=jnp.float32)

    def out_step(block_index, accum):
        scores, key_start = resp_scores(block_index)
        weights = jnp.exp(scores - log_total[..., None]).astype(jnp.bfloat16)
        values_block = lax.dynamic_slice_in_dim(values_r, key_start, shard_rows, 0)
        return accum + jnp.einsum(
            "tgs,sd->tgd", weights, values_block, preferred_element_type=jnp.float32
        )

    attended = lax.fori_loop(0, blocks, out_step, attended).astype(jnp.bfloat16)
    row_delta = jnp.sum(head_cot.astype(jnp.float32) * attended.astype(jnp.float32), axis=-1)
    dprobs_p = jnp.einsum("tgd,sd->tgs", head_cot, values_p, preferred_element_type=jnp.float32)
    dscores_p = (probs_p * (dprobs_p - row_delta[..., None])).astype(jnp.bfloat16)
    grad_query = jnp.einsum("tgs,sd->tgd", dscores_p, keys_p, preferred_element_type=jnp.float32)
    grad_kp = (
        jnp.einsum("tgs,tgd->sd", dscores_p, head_q, preferred_element_type=jnp.float32) * inv_root
    )
    grad_vp = jnp.einsum("tgs,tgd->sd", weights_p, head_cot, preferred_element_type=jnp.float32)

    def back_step(block_index, state):
        grad_accum, grad_kr, grad_vr = state
        scores, key_start = resp_scores(block_index)
        probs = jnp.exp(scores - log_total[..., None])
        weights = probs.astype(jnp.bfloat16)
        keys_block = lax.dynamic_slice_in_dim(keys_r, key_start, shard_rows, 0)
        values_block = lax.dynamic_slice_in_dim(values_r, key_start, shard_rows, 0)
        dprobs = jnp.einsum(
            "tgd,sd->tgs", head_cot, values_block, preferred_element_type=jnp.float32
        )
        dscores = (probs * (dprobs - row_delta[..., None])).astype(jnp.bfloat16)
        grad_accum = grad_accum + jnp.einsum(
            "tgs,sd->tgd", dscores, keys_block, preferred_element_type=jnp.float32
        )
        key_part = (
            jnp.einsum("tgs,tgd->sd", dscores, head_q, preferred_element_type=jnp.float32)
            * inv_root
        )
        value_part = jnp.einsum(
            "tgs,tgd->sd", weights, head_cot, preferred_element_type=jnp.float32
        )
        grad_kr = lax.dynamic_update_slice_in_dim(grad_kr, key_part, key_start, 0)
        grad_vr = lax.dynamic_update_slice_in_dim(grad_vr, value_part, key_start, 0)
        return (grad_accum, grad_kr, grad_vr)

    empty_rows = jnp.zeros(keys_r.shape, jnp.float32)
    grad_query, grad_kr, grad_vr = lax.fori_loop(
        0, blocks, back_step, (grad_query, empty_rows, empty_rows)
    )
    return (
        attended,
        (grad_query * inv_root).astype(jnp.bfloat16),
        grad_kp,
        grad_vp,
        grad_kr,
        grad_vr,
    )


def per_device(
    queries,
    resp_keys,
    resp_values,
    prefix_keys,
    prefix_values,
    grad_out,
    prompt_ids,
    prefix_lengths,
    resp_lengths,
):
    head_queries, head_cots, keys_local, values_local = (
        lax.all_to_all(queries, "mp", split_axis=2, concat_axis=1, tiled=True),
        lax.all_to_all(grad_out, "mp", split_axis=2, concat_axis=1, tiled=True),
        lax.all_to_all(resp_keys, "mp", split_axis=2, concat_axis=1, tiled=True),
        lax.all_to_all(resp_values, "mp", split_axis=2, concat_axis=1, tiled=True),
    )
    keys_resp, values_resp = (
        lax.all_gather(keys_local, "resp", axis=1, tiled=True),
        lax.all_gather(values_local, "resp", axis=1, tiled=True),
    )
    keys_prefix, values_prefix = (
        lax.all_gather(prefix_keys, "prefix", axis=1, tiled=True),
        lax.all_gather(prefix_values, "prefix", axis=1, tiled=True),
    )
    resp_count, shard_rows, local_heads, head_size = head_queries.shape
    kv_heads = keys_local.shape[2]
    group_size = local_heads // kv_heads
    resp_shards = lax.axis_size("resp")
    positions = lax.axis_index("resp") * shard_rows + jnp.arange(shard_rows, dtype=jnp.int32)
    grad_keys_prefix = jnp.zeros(keys_prefix.shape, jnp.float32)
    grad_values_prefix = jnp.zeros(values_prefix.shape, jnp.float32)
    attended_list = []
    grad_q_list = []
    grad_kr_list = []
    grad_vr_list = []
    for member in range(resp_count):
        global_index = lax.axis_index("prefix") * resp_count + member
        prompt = lax.dynamic_index_in_dim(prompt_ids, global_index, 0, keepdims=False)
        length = lax.dynamic_index_in_dim(resp_lengths, global_index, 0, keepdims=False)
        prefix_len = lax.dynamic_index_in_dim(prefix_lengths, prompt, 0, keepdims=False)
        live_rows = positions < length
        cot_member = jnp.where(
            live_rows[:, None, None], head_cots[member], jnp.zeros_like(head_cots[member])
        )
        keys_member = lax.dynamic_index_in_dim(keys_prefix, prompt, 0, keepdims=False)
        values_member = lax.dynamic_index_in_dim(values_prefix, prompt, 0, keepdims=False)
        attended_heads = []
        grad_q_heads = []
        grad_kr_heads = []
        grad_vr_heads = []
        for kv_head in range(kv_heads):
            first_q = kv_head * group_size
            attended, grad_query, grad_kp, grad_vp, grad_kr, grad_vr = head_pass(
                head_queries[member][:, first_q : first_q + group_size],
                cot_member[:, first_q : first_q + group_size],
                keys_member[:, kv_head],
                values_member[:, kv_head],
                keys_resp[member][:, kv_head],
                values_resp[member][:, kv_head],
                prefix_len,
                length,
                positions,
                resp_shards,
            )
            grad_keys_prefix = grad_keys_prefix.at[prompt, :, kv_head].add(grad_kp)
            grad_values_prefix = grad_values_prefix.at[prompt, :, kv_head].add(grad_vp)
            attended_heads.append(attended)
            grad_q_heads.append(grad_query)
            grad_kr_heads.append(grad_kr)
            grad_vr_heads.append(grad_vr)
        attended_list.append(jnp.concatenate(attended_heads, axis=1))
        grad_q_list.append(jnp.concatenate(grad_q_heads, axis=1))
        grad_kr_list.append(jnp.stack(grad_kr_heads, axis=1))
        grad_vr_list.append(jnp.stack(grad_vr_heads, axis=1))
    attended_all = jnp.stack(attended_list, axis=0)
    grad_q_all = jnp.stack(grad_q_list, axis=0)
    keys_summed, values_summed = (
        lax.psum_scatter(jnp.stack(grad_kr_list, axis=0), "resp", scatter_dimension=1, tiled=True),
        lax.psum_scatter(jnp.stack(grad_vr_list, axis=0), "resp", scatter_dimension=1, tiled=True),
    )
    slim_keys, slim_values = (
        lax.psum_scatter(grad_keys_prefix, ("prefix", "resp"), scatter_dimension=1, tiled=True),
        lax.psum_scatter(grad_values_prefix, ("prefix", "resp"), scatter_dimension=1, tiled=True),
    )
    d_prefix_keys, d_prefix_values = (
        lax.all_gather(slim_keys.astype(jnp.bfloat16), "resp", axis=1, tiled=True),
        lax.all_gather(slim_values.astype(jnp.bfloat16), "resp", axis=1, tiled=True),
    )
    attention, d_queries, d_resp_keys, d_resp_values = (
        lax.all_to_all(attended_all, "mp", split_axis=1, concat_axis=2, tiled=True),
        lax.all_to_all(grad_q_all, "mp", split_axis=1, concat_axis=2, tiled=True),
        lax.all_to_all(
            keys_summed.astype(jnp.bfloat16), "mp", split_axis=1, concat_axis=2, tiled=True
        ),
        lax.all_to_all(
            values_summed.astype(jnp.bfloat16), "mp", split_axis=1, concat_axis=2, tiled=True
        ),
    )
    return (attention, d_queries, d_resp_keys, d_resp_values, d_prefix_keys, d_prefix_values)


def solution(mesh):
    in_specs = (
        P("prefix", ("resp", "mp"), None, None),
        P("prefix", ("resp", "mp"), None, None),
        P("prefix", ("resp", "mp"), None, None),
        P(None, "prefix", "mp", None),
        P(None, "prefix", "mp", None),
        P("prefix", ("resp", "mp"), None, None),
        P(),
        P(),
        P(),
    )
    out_specs = (
        P("prefix", ("resp", "mp"), None, None),
        P("prefix", ("resp", "mp"), None, None),
        P("prefix", ("resp", "mp"), None, None),
        P("prefix", ("resp", "mp"), None, None),
        P(None, "prefix", "mp", None),
        P(None, "prefix", "mp", None),
    )
    return jax.shard_map(
        per_device, mesh=mesh, in_specs=in_specs, out_specs=out_specs, check_vma=False
    )
```

profile of v0, /device:TPU:1, one launch (start us, length us, event | category | flops | bytes accessed | tf_op | source)
XLA Modules:
  0.0 840.9 jit_solution(16780614319527301903)
XLA Ops:
  8.2 10.3 %all_to_all.138 = bf16[2,64,4,128]{3,1,0,2:T(8,128)(2,1)S(1)} all-to-all(bf16[2,64,4,128]{3,1,0,2:T(8,128)(2,1)S(1)} %copy.104), channel_id=1, replica_groups=mesh['prefix'=8,'resp'=8,'mp'=2] {'mp'}, dimensions={2} | all-to-all | bytes 262144 | tf_op jit(solution)/shard_map/all_to_all | solution.py:125
  20.2 7.2 all_to_all.139
  54.7 8.4 all-to-all-done.4
  71.7 35.6 %all-gather.5.cloned.1.call-done = bf16[2,2048,2,128]{3,2,1,0:T(2,128)(2,1)} async-done(((bf16[2,256,2,128]{3,2,1,0:T(2,128)(2,1)}), bf16[2,2048,2,128]{3,2,1,0:T(2,128)(2,1)}) %all-gather.5.cloned.1.call-update) | async-done | bytes 2097168 | tf_op jit(solution)/shard_map/all_gather | solution.py:133
  112.9 5.9 fusion.210
  118.8 15.3 %while.200 = (s32[]{:T(128)}, f32[128,8]{0,1:T(8,128)S(1)}, f32[128,8]{0,1:T(8,128)S(1)}, s32[]{:T(128)}, bf16[1024,128]{1,0:T(8,128)(2,1)}, /*index=5*/bf16[128...) while((s32[]{:T(128)}, f32[128,8]{0,1:T(8,128)S(1)}, ...), condition=%wide.region_5.6_spmd.clone, body=%wide.region_2.5_spmd.clone.sunk | while | flops 34245124 | bytes 1431983 | solution.py:48
  138.6 15.3 %while.202 = (s32[]{:T(128)}, f32[128,8]{0,1:T(8,128)S(1)}, f32[128,8]{0,1:T(8,128)S(1)}, s32[]{:T(128)}, bf16[1024,128]{1,0:T(8,128)(2,1)}, /*index=5*/bf16[128...) while((s32[]{:T(128)}, f32[128,8]{0,1:T(8,128)S(1)}, ...), condition=%wide.region_13.14_spmd.clone, body=%wide.region_10.13_spmd.clone.sunk | while | flops 34245124 | bytes 1431983 | solution.py:48
  162.5 15.5 %while.204 = (s32[]{:T(128)}, f32[128,8]{0,1:T(8,128)S(1)}, f32[128,8]{0,1:T(8,128)S(1)}, s32[]{:T(128)}, bf16[1024,128]{1,0:T(8,128)(2,1)}, /*index=5*/bf16[128...) while((s32[]{:T(128)}, f32[128,8]{0,1:T(8,128)S(1)}, ...), condition=%wide.region_21.22_spmd.clone, body=%wide.region_18.21_spmd.clone.sunk | while | flops 34245124 | bytes 1431983 | solution.py:48
  182.4 9.4 %while.206 = (s32[]{:T(128)}, f32[128,8]{0,1:T(8,128)S(1)}, f32[128,8]{0,1:T(8,128)S(1)}, s32[]{:T(128)}, bf16[1024,128]{1,0:T(8,128)(2,1)S(1)}, /*index=5*/bf16...) while((s32[]{:T(128)}, f32[128,8]{0,1:T(8,128)S(1)}, ...), condition=%wide.region_29.30_spmd.clone, body=%wide.region_26.29_spmd.clone.sunk | while | flops 34245124 | bytes 1431983 | solution.py:48
  194.9 6.5 fusion.256
  233.0 25.1 %while.203 = (s32[]{:T(128)}, f32[128,8,128]{2,0,1:T(8,128)}, s32[]{:T(128)}, bf16[1024,128]{1,0:T(8,128)(2,1)}, bf16[128,8,128]{2,0,1:T(8,128)(2,1)S(1)}, /*ind...) while((s32[]{:T(128)}, f32[128,8,128]{2,0,1:T(8,128)}, ...), condition=%wide.region_15.16_spmd.clone, body=%wide.region_14.15_spmd.clone.sunk | while | flops 67797512 | bytes 1416627 | solution.py:62
  258.1 16.4 %while.201 = (s32[]{:T(128)}, f32[128,8,128]{2,0,1:T(8,128)S(1)}, s32[]{:T(128)}, bf16[1024,128]{1,0:T(8,128)(2,1)}, bf16[128,8,128]{2,0,1:T(8,128)(2,1)S(1)}, /...) while((s32[]{:T(128)}, f32[128,8,128]{2,0,1:T(8,128)S(1)}, ...), condition=%wide.region_7.8_spmd.clone, body=%wide.region_6.7_spmd.clone.sunk | while | flops 67797512 | bytes 1416627 | solution.py:62
  297.6 24.9 %while.207 = (s32[]{:T(128)}, f32[128,8,128]{2,0,1:T(8,128)}, s32[]{:T(128)}, bf16[1024,128]{1,0:T(8,128)(2,1)S(1)}, bf16[128,8,128]{2,0,1:T(8,128)(2,1)S(1)}, /...) while((s32[]{:T(128)}, f32[128,8,128]{2,0,1:T(8,128)}, ...), condition=%wide.region_31.32_spmd.clone, body=%wide.region_30.31_spmd.clone.sunk | while | flops 67797512 | bytes 1416627 | solution.py:62
  322.5 16.5 %while.205 = (s32[]{:T(128)}, f32[128,8,128]{2,0,1:T(8,128)S(1)}, s32[]{:T(128)}, bf16[1024,128]{1,0:T(8,128)(2,1)}, bf16[128,8,128]{2,0,1:T(8,128)(2,1)S(1)}, /...) while((s32[]{:T(128)}, f32[128,8,128]{2,0,1:T(8,128)S(1)}, ...), condition=%wide.region_23.24_spmd.clone, body=%wide.region_22.23_spmd.clone.sunk | while | flops 67797512 | bytes 1416627 | solution.py:62
  364.8 52.9 %while.208 = (s32[]{:T(128)}, f32[128,8,128]{2,0,1:T(8,128)}, f32[1024,128]{1,0:T(8,128)}, f32[1024,128]{1,0:T(8,128)}, s32[]{:T(128)}, /*index=5*/bf16[1024,128...) while((s32[]{:T(128)}, f32[128,8,128]{2,0,1:T(8,128)}, ...), condition=%wide.region_34.35_spmd.clone, body=%wide.region_33.34_spmd.clone.sunk | while | flops 168870400 | bytes 4729319 | solution.py:98
  419.4 44.2 %while.209 = (s32[]{:T(128)}, f32[128,8,128]{2,0,1:T(8,128)S(1)}, f32[1024,128]{1,0:T(8,128)}, f32[1024,128]{1,0:T(8,128)}, s32[]{:T(128)}, /*index=5*/bf16[1024...) while((s32[]{:T(128)}, f32[128,8,128]{2,0,1:T(8,128)S(1)}, ...), condition=%wide.region_37.38_spmd.clone, body=%wide.region_36.37_spmd.clone.sunk | while | flops 168870400 | bytes 4729319 | solution.py:98
  465.3 53.1 %while.210 = (s32[]{:T(128)}, f32[128,8,128]{2,0,1:T(8,128)}, f32[1024,128]{1,0:T(8,128)}, f32[1024,128]{1,0:T(8,128)}, s32[]{:T(128)}, /*index=5*/bf16[1024,128...) while((s32[]{:T(128)}, f32[128,8,128]{2,0,1:T(8,128)}, ...), condition=%wide.region_40.41_spmd.clone, body=%wide.region_39.40_spmd.clone.sunk | while | flops 168870400 | bytes 4729319 | solution.py:98
  519.3 27.4 %while.211 = (s32[]{:T(128)}, f32[128,8,128]{2,0,1:T(8,128)S(1)}, f32[1024,128]{1,0:T(8,128)S(1)}, f32[1024,128]{1,0:T(8,128)}, s32[]{:T(128)}, /*index=5*/bf16[...) while((s32[]{:T(128)}, f32[128,8,128]{2,0,1:T(8,128)S(1)}, ...), condition=%wide.region_43.44_spmd.clone, body=%wide.region_42.43_spmd.clone.sunk | while | flops 168870400 | bytes 4729319 | solution.py:98
  558.4 64.0 %all-reduce.4 = (bf16[2,1024,2,128]{3,2,0,1:T(2,128)(2,1)}, bf16[2,1024,2,128]{3,2,0,1:T(2,128)(2,1)}) all-reduce(f32[2,1024,2,128]{3,2,0,1:T(2,128)} %pad_maximum_fusion, f32[2,1024,2,128]{3,2,0,1:T(2,128)} %pad_maximum_fusion.1), channel_id=2, replica_groups=mesh['prefix'=8,'resp'=8,'mp'=2] {'resp'}, use_global_device_ids=true, to_apply=%region_44.45.clone | all-reduce | flops 1048576 | bytes 6291456
  648.7 9.6 %all-to-all-done.5 = bf16[2,128,16,128]{3,2,0,1:T(8,128)(2,1)S(1)} async-done(((bf16[2,128,16,128]{3,2,0,1:T(8,128)(2,1)}), bf16[2,128,16,128]{3,2,0,1:T(8,128)(2,1)S(1)}, u32[]{:S(2)}, u32[]{:S(2)}) %all-to-all-start.5) | async-done | bytes 1048608 | tf_op jit(solution)/shard_map/all_to_all | solution.py:202
  664.6 9.0 %all-to-all-done.3 = bf16[2,128,16,128]{3,2,0,1:T(8,128)(2,1)S(1)} async-done(((bf16[2,128,16,128]{3,2,0,1:T(8,128)(2,1)}), bf16[2,128,16,128]{3,2,0,1:T(8,128)(2,1)S(1)}, u32[]{:S(2)}, u32[]{:S(2)}) %all-to-all-start.3) | async-done | bytes 1048608 | tf_op jit(solution)/shard_map/all_to_all | solution.py:201
  675.6 19.3 %all_gather.23 = bf16[2,256,2,128]{3,1,2,0:T(8,128)(2,1)S(1)} all-gather(bf16[2,32,2,128]{3,1,2,0:T(8,128)(2,1)S(1)} %convert_element_type.195), channel_id=1, replica_groups=mesh['prefix'=8,'resp'=8,'mp'=2] {'resp'}, dimensions={1}, use_global_device_ids=true | all-gather | bytes 294912 | tf_op jit(solution)/shard_map/all_gather | solution.py:198
  695.9 117.0 %reduce-scatter.3.cloned.1.call-done = f32[2,32,2,128]{3,1,2,0:T(8,128)} async-done(((f32[2,2048,2,128]{3,1,2,0:T(8,128)}), f32[2,32,2,128]{3,1,2,0:T(8,128)}) %reduce-scatter.3.cloned.1.call-update) | async-done | bytes 65552 | tf_op jit(solution)/shard_map/reduce_scatter | solution.py:193
  813.7 18.9 %all_gather.22 = bf16[2,256,2,128]{3,1,2,0:T(8,128)(2,1)S(1)} all-gather(bf16[2,32,2,128]{3,1,2,0:T(8,128)(2,1)S(1)} %convert_element_type.194), channel_id=1, replica_groups=mesh['prefix'=8,'resp'=8,'mp'=2] {'resp'}, dimensions={1}, use_global_device_ids=true | all-gather | bytes 294912 | tf_op jit(solution)/shard_map/all_gather | solution.py:197
  (864 shorter events, 503.5 us)
Async XLA Ops:
  7.2 38.9 %copy-start.34 = (s32[4]{0:T(128)S(1)}, s32[4]{0:T(128)}, u32[]{:S(2)}) copy-start(s32[4]{0:T(128)} %constant.766.clone.1) | copy-start | bytes 52
  7.2 45.2 %copy-start.35 = (u32[128]{0:T(128)S(1)}, u32[128]{0:T(128)}, u32[]{:S(2)}) copy-start(u32[128]{0:T(128)} %constant.775) | copy-start | bytes 1540
  7.2 36.3 %copy-start.33 = (s32[2]{0:T(128)S(1)}, s32[2]{0:T(128)}, u32[]{:S(2)}) copy-start(s32[2]{0:T(128)} %param.56) | copy-start | bytes 28
  7.2 58.0 %all-gather.7.cloned.1.call-start = ((), (), s32[]{:S(2)}) async-start(), calls=%async_computation.11 | async-start | bytes 1179648 | tf_op jit(solution)/shard_map/all_gather | solution.py:129
  19.2 50.2 %all-gather.11.cloned.1.call-start = ((), (), s32[]{:S(2)}) async-start(), calls=%async_computation.13 | async-start | bytes 1179648 | tf_op jit(solution)/shard_map/all_gather | solution.py:130
  28.1 79.2 %all-gather.5.cloned.1.call-start = ((), (), s32[]{:S(2)}) async-start(), calls=%async_computation.10 | async-start | bytes 2359296 | tf_op jit(solution)/shard_map/all_gather | solution.py:133
  31.4 16.1 %all-to-all-start = ((bf16[2,64,32,128]{3,1,0,2:T(8,128)(2,1)}), bf16[2,64,32,128]{3,1,0,2:T(8,128)(2,1)S(1)}, u32[]{:S(2)}, u32[]{:S(2)}) async-start(bf16[2,64,32,128]{3,1,0,2:T(8,128)(2,1)} %copy.102), calls=%async_computation | async-start | bytes 2097152 | tf_op jit(solution)/shard_map/all_to_all | solution.py:123
  35.0 156.7 %all-gather.9.cloned.1.call-start = ((), (), s32[]{:S(2)}) async-start(), calls=%async_computation.12 | async-start | bytes 2359296 | tf_op jit(solution)/shard_map/all_gather | solution.py:134
  47.5 15.5 %all-to-all-start.4 = ((bf16[2,64,32,128]{3,1,0,2:T(8,128)(2,1)}), bf16[2,64,32,128]{3,1,0,2:T(8,128)(2,1)S(1)}, u32[]{:S(2)}, u32[]{:S(2)}) async-start(bf16[2,64,32,128]{3,1,0,2:T(8,128)(2,1)} %copy.117), calls=%async_computation.4 | async-start | bytes 2097152 | tf_op jit(solution)/shard_map/all_to_all | solution.py:124
  51.7 623.0 %reduce-scatter.5.cloned.1.call-start = ((), (), s32[]{:S(2)}) async-start(), calls=%async_computation.15 | async-start | bytes 4259840 | tf_op jit(solution)/shard_map/reduce_scatter | solution.py:194
  53.8 16.8 %copy-start.10 = (bf16[1,2,64,16,128]{4,2,1,3,0:T(8,128)(2,1)}, bf16[1,2,64,16,128]{4,2,1,3,0:T(8,128)(2,1)S(1)}, u32[]{:S(2)}) copy-start(bf16[1,2,64,16,128]{4,2,1,3,0:T(8,128)(2,1)S(1)} %get-tuple-element.2595) | copy-start | bytes 1572868
  162.5 19.9 %copy-start.16 = (bf16[1024,128]{1,0:T(8,128)(2,1)S(1)}, bf16[1024,128]{1,0:T(8,128)(2,1)}, u32[]{:S(2)}) copy-start(bf16[1024,128]{1,0:T(8,128)(2,1)} %get-tuple-element.3637) | copy-start | bytes 786436
  194.9 9.0 %copy-start.28 = (bf16[1,2048,2,128]{3,1,2,0:T(8,128)(2,1)}, bf16[1,2048,2,128]{3,1,2,0:T(8,128)(2,1)S(1)}, u32[]{:S(2)}) copy-start(bf16[1,2048,2,128]{3,1,2,0:T(8,128)(2,1)S(1)} %copy.178) | copy-start | bytes 3145732
  194.9 9.1 %slice-start.8 = ((s8[8388608]{0:T(1024)(128)(4,1)}), s8[4194304]{0:T(1024)(128)(4,1)S(1)}, s32[]{:S(2)}) async-start(s8[8388608]{0:T(1024)(128)(4,1)} %bitcast.779), calls=%async_computation.24 | async-start | bytes 8388608
  232.9 580.0 %reduce-scatter.3.cloned.1.call-start = ((), (), s32[]{:S(2)}) async-start(), calls=%async_computation.14 | async-start | bytes 4259840 | tf_op jit(solution)/shard_map/reduce_scatter | solution.py:193
  551.9 76.0 %copy-start.1 = (f32[128,8,128]{2,0,1:T(8,128)S(1)}, f32[128,8,128]{2,0,1:T(8,128)}, u32[]{:S(2)}) copy-start(f32[128,8,128]{2,0,1:T(8,128)} %get-tuple-element.1974) | copy-start | bytes 1572868
  554.2 74.5 %copy-start = (f32[128,8,128]{2,0,1:T(8,128)S(1)}, f32[128,8,128]{2,0,1:T(8,128)}, u32[]{:S(2)}) copy-start(f32[128,8,128]{2,0,1:T(8,128)} %get-tuple-element.1976) | copy-start | bytes 1572868
  558.4 87.4 %copy-start.30 = (bf16[128,8,128]{2,0,1:T(8,128)(2,1)S(1)}, bf16[128,8,128]{2,0,1:T(8,128)(2,1)}, u32[]{:S(2)}) copy-start(bf16[128,8,128]{2,0,1:T(8,128)(2,1)} %get-tuple-element.2550) | copy-start | bytes 786436
  558.4 87.4 %copy-start.31 = (bf16[128,8,128]{2,0,1:T(8,128)(2,1)S(1)}, bf16[128,8,128]{2,0,1:T(8,128)(2,1)}, u32[]{:S(2)}) copy-start(bf16[128,8,128]{2,0,1:T(8,128)(2,1)} %get-tuple-element.2551) | copy-start | bytes 786436
  558.4 87.5 %copy-start.32 = (bf16[128,8,128]{2,0,1:T(8,128)(2,1)S(1)}, bf16[128,8,128]{2,0,1:T(8,128)(2,1)}, u32[]{:S(2)}) copy-start(bf16[128,8,128]{2,0,1:T(8,128)(2,1)} %get-tuple-element.2552) | copy-start | bytes 786436
  624.1 9.3 %all-to-all-start.6 = ((bf16[2,128,2,128]{3,2,0,1:T(2,128)(2,1)}), bf16[2,128,2,128]{3,2,0,1:T(2,128)(2,1)S(1)}, u32[]{:S(2)}, u32[]{:S(2)}) async-start(bf16[2,128,2,128]{3,2,0,1:T(2,128)(2,1)} %dynamic-slice_convert_fusion.1), calls=%async_computation.6 | async-start | bytes 262144 | tf_op jit(solution)/shard_map/all_to_all | solution.py:203
  633.4 8.8 %all-to-all-start.7 = ((bf16[2,128,2,128]{3,2,0,1:T(2,128)(2,1)}), bf16[2,128,2,128]{3,2,0,1:T(2,128)(2,1)S(1)}, u32[]{:S(2)}, u32[]{:S(2)}) async-start(bf16[2,128,2,128]{3,2,0,1:T(2,128)(2,1)} %dynamic-slice_convert_fusion), calls=%async_computation.7 | async-start | bytes 262144 | tf_op jit(solution)/shard_map/all_to_all | solution.py:206
  642.3 16.1 %all-to-all-start.5 = ((bf16[2,128,16,128]{3,2,0,1:T(8,128)(2,1)}), bf16[2,128,16,128]{3,2,0,1:T(8,128)(2,1)S(1)}, u32[]{:S(2)}, u32[]{:S(2)}) async-start(bf16[2,128,16,128]{3,2,0,1:T(8,128)(2,1)} %pad_maximum_fusion.3), calls=%async_computation.5 | async-start | bytes 2097152 | tf_op jit(solution)/shard_map/all_to_all | solution.py:202
  658.3 15.3 %all-to-all-start.3 = ((bf16[2,128,16,128]{3,2,0,1:T(8,128)(2,1)}), bf16[2,128,16,128]{3,2,0,1:T(8,128)(2,1)S(1)}, u32[]{:S(2)}, u32[]{:S(2)}) async-start(bf16[2,128,16,128]{3,2,0,1:T(8,128)(2,1)} %copy.115), calls=%async_computation.3 | async-start | bytes 2097152 | tf_op jit(solution)/shard_map/all_to_all | solution.py:201
  (34 other events, 185.4 us)
Sparse Core Ops, SparseCore 0:
  19.3 24.5 all-gather.6
  46.2 23.1 all-gather.10
  71.1 36.1 all-gather.4
  108.7 40.6 all-gather.8
  233.1 288.7 reduce-scatter.4
  524.2 288.6 reduce-scatter.2
where the time goes:
time: 854 us; the launch traced here: 841 us
  matrix products  328 us (38%)
  waiting for transfers between devices  189 us (22%)
  blocking collectives  120 us (14%)
  other arithmetic  108 us (13%)
  local copies, waits for them, and re-layouts  47.9 us (6%)
  starting transfers between devices  22.4 us (3%)
  between operations  20.1 us (2%)
    reduce_scatter x1, waiting for transfers between devices, per_device(): lax.psum_scatter(grad_keys_prefix, ('prefix', 'resp'), scatter_dimension=...  117 us
    unnamed x1, blocking collectives  64 us
    lt x96, other arithmetic, block_scores(): key_pos[None, :] < length  61 us
    dot_general x32, matrix products, out_step(): jnp.einsum('tgs,sd->tgd', weights, values_block, preferred_element_type=j...  58.1 us
    dot_general x64, matrix products, block_scores(): jnp.einsum('tgd,sd->tgs', head_q, keys_block, preferred_element_type=jnp....  52.6 us
    dot_general x32, matrix products, back_step(): jnp.einsum('tgs,sd->tgd', dscores, keys_block, preferred_element_type=jnp...  44.5 us
    all_gather x1, waiting for transfers between devices, per_device(): lax.all_gather(prefix_keys, 'prefix', axis=1, tiled=True)  35.6 us
    dot_general x32, matrix products, back_step(): jnp.einsum('tgd,sd->tgs', head_cot, values_block, preferred_element_type=...  31.8 us
  transfers between devices with their start and end apart: 12, of which 8 were waited for; matrix products, arithmetic and copies ran while one was open for 52% of the time, Pallas kernels for 0%

commit v1 on v0

v1 whole, which is shorter than its diff:
```python
import math
import jax, jax.numpy as jnp
from jax import lax
from jax.sharding import PartitionSpec as P
from jax.experimental import pallas as pl
from jax.experimental.pallas import tpu as pltpu

HD=128; PRE=2048; RL=1024; T=128; G=8; R=T*G
ROWS=2*PRE+2*RL
NT=(((1,),(1,)),((),()))
NN=(((1,),(0,)),((),()))
TN=(((0,),(0,)),((),()))
def dot(a,b,dn): return lax.dot_general(a,b,dn,preferred_element_type=jnp.float32)

def attend(KB=256, RC=256, variant="wt"):
    C2=math.log2(math.e)/math.sqrt(HD); INV=1/math.sqrt(HD)
    def kernel(meta, q_ref, c_ref, k_ref, v_ref, o_ref, dq_ref, dk_ref, dv_ref,
               qhl, qr, dr, S, Pm, mx, ls, oacc, dqacc, dkacc, dvacc, ocat, dqcat):
        pos0=meta[0]
        dkacc[...]=jnp.zeros_like(dkacc); dvacc[...]=jnp.zeros_like(dvacc)
        def prep(b, _):
            for tc in range(0,T,32):
                qf=q_ref[b,pl.ds(tc,32)].astype(jnp.float32)
                for h in range(2):
                    x=qf[:,h*G:(h+1)*G].reshape(32*G,HD)
                    rows=pl.ds(tc*G,32*G)
                    qr[h,b,rows]=x.astype(jnp.bfloat16)
                    xs=x*C2
                    hi=xs.astype(jnp.bfloat16)
                    lo=(xs-hi.astype(jnp.float32)).astype(jnp.bfloat16)
                    qhl[h,b,rows,0:HD]=hi
                    qhl[h,b,rows,HD:]=lo
            return 0
        lax.fori_loop(0,2,prep,0)
        def group(g,_):
            h=g//2; b=g%2
            prompt=meta[1+b]; length=meta[3+b]; plen=meta[5+b]
            npre=(plen+KB-1)//KB
            rk=jnp.minimum(pos0+T,length)
            nres=(rk+KB-1)//KB
            nblk=npre+nres
            def place(i):
                isp=i<npre
                j=i-npre
                row=jnp.where(isp, prompt*PRE+i*KB, 2*PRE+b*RL+j*KB)
                return isp, j, pl.multiple_of(row,KB)
            mx[...]=jnp.full_like(mx,-jnp.inf)
            ls[...]=jnp.zeros_like(ls)
            oacc[...]=jnp.zeros_like(oacc)
            def passA(i,_):
                isp,j,row=place(i)
                kb=k_ref[h,pl.ds(row,KB)]
                kk=jnp.concatenate([kb,kb],axis=1)
                col=lax.broadcasted_iota(jnp.int32,(RC,KB),1)
                base=jnp.where(isp,i*KB,j*KB)
                for rc in range(0,R,RC):
                    s=dot(qhl[h,b,pl.ds(rc,RC)],kk,NT)
                    t=pos0+rc//G+lax.broadcasted_iota(jnp.int32,(RC,1),0)//G
                    lim=jnp.where(isp,plen-1,jnp.minimum(t,length-1))-base
                    s=jnp.where(col<=lim,s,-1e30)
                    S[pl.ds(rc,RC),pl.ds(pl.multiple_of(i*KB,KB),KB)]=s
                    m=mx[pl.ds(rc,RC)]
                    for c in range(0,KB,128): m=jnp.maximum(m,s[:,c:c+128])
                    mx[pl.ds(rc,RC)]=m
                return 0
            lax.fori_loop(0,nblk,passA,0)
            for rc in range(0,R,RC):
                m=jnp.max(mx[pl.ds(rc,RC)],axis=1,keepdims=True)
                mx[pl.ds(rc,RC)]=jnp.broadcast_to(m,(RC,128))
            def passB(i,_):
                isp,j,row=place(i)
                vb=v_ref[h,pl.ds(row,KB)]
                for rc in range(0,R,RC):
                    m=mx[pl.ds(rc,RC)]
                    s=S[pl.ds(rc,RC),pl.ds(pl.multiple_of(i*KB,KB),KB)]
                    ps=[]
                    l=ls[pl.ds(rc,RC)]
                    for c in range(0,KB,128):
                        p=jnp.exp2(s[:,c:c+128]-m)
                        l=l+p
                        ps.append(p.astype(jnp.bfloat16))
                    ls[pl.ds(rc,RC)]=l
                    pb=jnp.concatenate(ps,axis=1)
                    Pm[pl.ds(rc,RC),pl.ds(pl.multiple_of(i*KB,KB),KB)]=pb
                    oacc[pl.ds(rc,RC)]+=dot(pb,vb,NN)
                return 0
            lax.fori_loop(0,nblk,passB,0)
            for rc in range(0,R,RC):
                rows=pl.ds(rc,RC)
                tr=pl.ds(rc//G,RC//G)
                l=jnp.sum(ls[rows],axis=1,keepdims=True)
                il=1.0/l
                o=(oacc[rows]*il).astype(jnp.bfloat16).astype(jnp.float32)
                ocat[h,b,rows]=o
                d=c_ref[b,tr].astype(jnp.float32)
                d=jnp.where(h==0,d[:,:G],d[:,G:]).reshape(RC,HD)
                t=pos0+rc//G+lax.broadcasted_iota(jnp.int32,(RC,1),0)//G
                d=jnp.where(t<length,d,0.0)
                delta=jnp.sum(d*o,axis=1,keepdims=True)
                dr[rows]=(d*il).astype(jnp.bfloat16)
                mx[rows]=jnp.broadcast_to(delta*il,(RC,128))
            dqacc[...]=jnp.zeros_like(dqacc)
            def passC(i,_):
                isp,j,row=place(i)
                vb=v_ref[h,pl.ds(row,KB)]
                kb=k_ref[h,pl.ds(row,KB)]
                dss=[]
                cs=pl.ds(pl.multiple_of(i*KB,KB),KB)
                for rc in range(0,R,RC):
                    rows=pl.ds(rc,RC)
                    dp=dot(dr[rows],vb,NT)
                    p=Pm[rows,cs].astype(jnp.float32)
                    dl=mx[rows]
                    ds=jnp.concatenate([p[:,c:c+128]*(dp[:,c:c+128]-dl) for c in range(0,KB,128)],axis=1).astype(jnp.bfloat16)
                    dqacc[rows]+=dot(ds,kb,NN)
                    dss.append(ds)
                ds=jnp.concatenate(dss,axis=0)
                if variant=="tn":
                    dkacc[h,pl.ds(row,KB)]+=dot(ds,qr[h,b],TN)
                    dvacc[h,pl.ds(row,KB)]+=dot(Pm[:,cs],dr[...],TN)
                else:
                    dkacc[h,pl.ds(row,KB)]+=dot(qr[h,b],ds,TN).T
                    dvacc[h,pl.ds(row,KB)]+=dot(dr[...],Pm[:,cs],TN).T
                return 0
            lax.fori_loop(0,jnp.where(length>pos0,nblk,0),passC,0)
            for rc in range(0,R,RC):
                dqcat[h,b,pl.ds(rc,RC)]=dqacc[pl.ds(rc,RC)]*INV
            return 0
        lax.fori_loop(0,4,group,0)
        def fin(b,_):
            for tc in range(0,T,32):
                rows=pl.ds(tc*G,32*G)
                for src,dst in ((ocat,o_ref),(dqcat,dq_ref)):
                    a=jnp.concatenate([src[h,b,rows].reshape(32,G,HD) for h in range(2)],axis=1)
                    dst[b,pl.ds(tc,32)]=a.astype(jnp.bfloat16)
            return 0
        lax.fori_loop(0,2,fin,0)
        def finkv(i,_):
            for h in range(2):
                rows=pl.ds(pl.multiple_of(i*512,512),512)
                dk_ref[h,rows]=(dkacc[h,rows]*INV).astype(jnp.bfloat16)
                dv_ref[h,rows]=dvacc[h,rows].astype(jnp.bfloat16)
            return 0
        lax.fori_loop(0,ROWS//512,finkv,0)
    bf=jnp.bfloat16; f32=jnp.float32
    V=pl.BlockSpec(memory_space=pltpu.VMEM)
    scratch=[pltpu.VMEM((2,2,R,2*HD),bf),pltpu.VMEM((2,2,R,HD),bf),pltpu.VMEM((R,HD),bf),
             pltpu.VMEM((R,3072),f32),pltpu.VMEM((R,3072),bf),pltpu.VMEM((R,128),f32),pltpu.VMEM((R,128),f32),
             pltpu.VMEM((R,HD),f32),pltpu.VMEM((R,HD),f32),pltpu.VMEM((2,ROWS,HD),f32),pltpu.VMEM((2,ROWS,HD),f32),
             pltpu.VMEM((2,2,R,HD),f32),pltpu.VMEM((2,2,R,HD),f32)]
    return pl.pallas_call(kernel,
        out_shape=[jax.ShapeDtypeStruct((2,T,16,HD),bf),jax.ShapeDtypeStruct((2,T,16,HD),bf),
                   jax.ShapeDtypeStruct((2,ROWS,HD),bf),jax.ShapeDtypeStruct((2,ROWS,HD),bf)],
        in_specs=[pl.BlockSpec(memory_space=pltpu.SMEM),V,V,V,V],out_specs=[V]*4,
        scratch_shapes=scratch,
        compiler_params=pltpu.CompilerParams(vmem_limit_bytes=60*2**20))


def per_device(queries, resp_keys, resp_values, prefix_keys, prefix_values, grad_out, prompt_ids, prefix_lengths, resp_lengths):
    q = lax.all_to_all(queries, "mp", split_axis=2, concat_axis=1, tiled=True)
    c = lax.all_to_all(grad_out, "mp", split_axis=2, concat_axis=1, tiled=True)
    kv = jnp.stack([resp_keys, resp_values])
    kv = lax.all_to_all(kv, "mp", split_axis=3, concat_axis=2, tiled=True)
    kv = lax.all_gather(kv.transpose(0, 3, 1, 2, 4), "resp", axis=3, tiled=True)
    pre = jnp.stack([prefix_keys, prefix_values]).transpose(0, 3, 1, 2, 4)
    pre = lax.all_gather(pre, "prefix", axis=3, tiled=True)
    flat = jnp.concatenate([pre.reshape(2, 2, 2 * PRE, HD), kv.reshape(2, 2, 2 * RL, HD)], axis=2)
    first = lax.axis_index("prefix") * 2
    prompts = lax.dynamic_slice_in_dim(prompt_ids, first, 2)
    lengths = lax.dynamic_slice_in_dim(resp_lengths, first, 2)
    pos0 = lax.axis_index("resp") * T
    meta = jnp.concatenate([pos0[None], prompts, lengths, prefix_lengths[prompts], jnp.zeros((1,), jnp.int32)]).astype(jnp.int32)
    o, dq, dk, dv = attend()(meta, q, c, flat[0], flat[1])
    terms = jnp.stack([dk, dv])
    rt = terms[:, :, 2 * PRE :].reshape(2, 2, 2, 8, T, HD)
    rt = lax.all_to_all(rt, "resp", split_axis=3, concat_axis=3, tiled=True)
    rt = jnp.sum(rt.astype(jnp.float32), axis=3).astype(jnp.bfloat16)
    rt = rt.transpose(0, 2, 3, 1, 4)
    rt = lax.all_to_all(rt, "mp", split_axis=2, concat_axis=3, tiled=True)
    pt = terms[:, :, : 2 * PRE].reshape(2, 2, 2, 64, 32, HD)
    pt = lax.all_to_all(pt, ("prefix", "resp"), split_axis=3, concat_axis=3, tiled=True)
    pt = jnp.sum(pt.astype(jnp.float32), axis=3).astype(jnp.bfloat16)
    pt = lax.all_gather(pt, "resp", axis=3, tiled=True).transpose(0, 2, 3, 1, 4)
    attention = lax.all_to_all(o, "mp", split_axis=1, concat_axis=2, tiled=True)
    d_queries = lax.all_to_all(dq, "mp", split_axis=1, concat_axis=2, tiled=True)
    return (attention, d_queries, rt[0], rt[1], pt[0], pt[1])


def solution(mesh):
    rows = P("prefix", ("resp", "mp"), None, None)
    pre = P(None, "prefix", "mp", None)
    return jax.shard_map(
        per_device,
        mesh=mesh,
        in_specs=(rows, rows, rows, pre, pre, rows, P(), P(), P()),
        out_specs=(rows, rows, rows, rows, pre, pre),
        check_vma=False,
    )
```

time: 854 us -> 347 us (0.41); the launches traced: 841 us -> 346 us
  matrix products: 328 us -> 0 us
  blocking collectives: 120 us -> 26.6 us
  other arithmetic: 108 us -> 16.3 us
  Pallas kernels: 0 us -> 51.4 us
  waiting for transfers between devices: 189 us -> 153 us
  starting transfers between devices: 22.4 us -> 52.3 us
  local copies, waits for them, and re-layouts: 47.9 us -> 32.8 us
    dot_general x248 -> x0, matrix products: 328 us -> none  [the longest x32 58.1 us: out_step(): jnp.einsum('tgs,sd->tgd', weights, values_block, preferred_element_type=j...]
    all_to_all x6 -> x7, waiting for transfers between devices: 33.7 us -> 153 us  [the longest x1 49.2 us: per_device(): q = lax.all_to_all(queries, 'mp', split_axis=2, concat_axis=1, tiled=True)]
    reduce_scatter x2 -> x0, waiting for transfers between devices: 117 us -> none  [the longest x1 117 us: per_device(): lax.psum_scatter(grad_keys_prefix, ('prefix', 'resp'), scatter_dimension=...]
    unnamed x1 -> x0, blocking collectives: 64 us -> none
    lt x100 -> x0, other arithmetic: 63.5 us -> none  [the longest x96 61 us: block_scores(): key_pos[None, :] < length]
    pallas_call x0 -> x1, Pallas kernels: none -> 51.4 us  [per_device(): o, dq, dk, dv = attend()(meta, q, c, flat[0], flat[1])]
    all_gather x4 -> x2, waiting for transfers between devices: 37.5 us -> 0.01 us  [the longest x1 0.01 us: per_device(): pre = lax.all_gather(pre, 'prefix', axis=3, tiled=True)]
    all_to_all x6 -> x7, starting transfers between devices: 22.2 us -> 52.2 us  [the longest x1 21.2 us: per_device(): lax.all_to_all(pt, ('prefix', 'resp'), split_axis=3, concat_axis=3, tiled...]
  transfers between devices with their start and end apart: 12 -> 9, of which waited for: 8 -> 6; matrix products, arithmetic and copies ran while one was open for 52% -> 10% of each run, Pallas kernels for 0% -> 0%
where the time goes in v1:
time: 347 us; the launch traced here: 346 us
  waiting for transfers between devices  153 us (44%)
  starting transfers between devices  52.3 us (15%)
  Pallas kernels  51.4 us (15%)
  local copies, waits for them, and re-layouts  32.8 us (9%)
  blocking collectives  26.6 us (8%)
  other arithmetic  16.3 us (5%)
  between operations  14.2 us (4%)
    pallas_call x1, Pallas kernels, per_device(): o, dq, dk, dv = attend()(meta, q, c, flat[0], flat[1])  51.4 us
    all_to_all x1, waiting for transfers between devices, per_device(): q = lax.all_to_all(queries, 'mp', split_axis=2, concat_axis=1, tiled=True)  49.2 us
    all_to_all x1, waiting for transfers between devices, per_device(): lax.all_to_all(pt, ('prefix', 'resp'), split_axis=3, concat_axis=3, tiled...  45.4 us
    all_to_all x1, waiting for transfers between devices, per_device(): rt = lax.all_to_all(rt, 'resp', split_axis=3, concat_axis=3, tiled=True)  24.1 us
    all_to_all x1, starting transfers between devices, per_device(): lax.all_to_all(pt, ('prefix', 'resp'), split_axis=3, concat_axis=3, tiled...  21.2 us
    all_gather x1, blocking collectives, per_device(): pt = lax.all_gather(pt, 'resp', axis=3, tiled=True).transpose(0, 2, 3, 1, 4)  15.5 us
    all_to_all x1, waiting for transfers between devices, per_device(): c = lax.all_to_all(grad_out, 'mp', split_axis=2, concat_axis=1, tiled=True)  11.6 us
    all_to_all x1, starting transfers between devices, per_device(): rt = lax.all_to_all(rt, 'resp', split_axis=3, concat_axis=3, tiled=True)  11.5 us
  transfers between devices with their start and end apart: 9, of which 6 were waited for; matrix products, arithmetic and copies ran while one was open for 10% of the time, Pallas kernels for 0%

profile of v1, /device:TPU:1, one launch (start us, length us, event | category | flops | bytes accessed | tf_op | source)
XLA Modules:
  0.0 346.2 jit_solution(9281794709599382620)
XLA Ops:
  7.2 2.8 maximum_bitcast_fusion
  11.2 11.0 %all_to_all.115 = bf16[2,2,64,4,128]{4,2,1,0,3:T(8,128)(2,1)S(1)} all-to-all(bf16[2,2,64,4,128]{4,2,1,0,3:T(8,128)(2,1)S(1)} %pad_maximum_fusion.3), channel_id=1, replica_groups=mesh['prefix'=8,'resp'=8,'mp'=2] {'mp'}, dimensions={3} | all-to-all | bytes 524288 | tf_op jit(solution)/shard_map/all_to_all | solution.py:163
  24.4 3.6 %all-to-all-start = ((bf16[2,64,32,128]{3,1,0,2:T(8,128)(2,1)}), bf16[2,64,32,128]{3,1,0,2:T(8,128)(2,1)S(1)}, u32[]{:S(2)}, u32[]{:S(2)}) async-start(bf16[2,64,32,128]{3,1,0,2:T(8,128)(2,1)} %copy.37), calls=%async_computation | async-start | bytes 2097152 | tf_op jit(solution)/shard_map/all_to_all | solution.py:160
  29.3 49.2 %all-to-all-done = bf16[2,64,32,128]{3,1,0,2:T(8,128)(2,1)S(1)} async-done(((bf16[2,64,32,128]{3,1,0,2:T(8,128)(2,1)}), bf16[2,64,32,128]{3,1,0,2:T(8,128)(2,1)S(1)}, u32[]{:S(2)}, u32[]{:S(2)}) %all-to-all-start) | async-done | bytes 1048608 | tf_op jit(solution)/shard_map/all_to_all | solution.py:160
  78.5 3.6 %all-to-all-start.1 = ((bf16[2,64,32,128]{3,1,0,2:T(8,128)(2,1)}), bf16[2,64,32,128]{3,1,0,2:T(8,128)(2,1)S(1)}, u32[]{:S(2)}, u32[]{:S(2)}) async-start(bf16[2,64,32,128]{3,1,0,2:T(8,128)(2,1)} %copy.39), calls=%async_computation.1 | async-start | bytes 2097152 | tf_op jit(solution)/shard_map/all_to_all | solution.py:161
  85.2 11.6 %all-to-all-done.1 = bf16[2,64,32,128]{3,1,0,2:T(8,128)(2,1)S(1)} async-done(((bf16[2,64,32,128]{3,1,0,2:T(8,128)(2,1)}), bf16[2,64,32,128]{3,1,0,2:T(8,128)(2,1)S(1)}, u32[]{:S(2)}, u32[]{:S(2)}) %all-to-all-start.1) | async-done | bytes 1048608 | tf_op jit(solution)/shard_map/all_to_all | solution.py:161
  98.4 4.7 %copy.41 = bf16[2,2,2,2048,128]{4,3,2,1,0:T(8,128)(2,1)} copy(bf16[2,2,2,2048,128]{4,1,3,2,0:T(2,128)(2,1)} %all-gather.3.cloned.1.call-done) | data formatting | bytes 8388608 | tf_op jit(solution)/shard_map/all_gather | solution.py:166
  103.1 4.7 %fusion.2 = (bf16[2,6144,128]{2,1,0:T(8,128)(2,1)}, bf16[2,6144,128]{2,1,0:T(8,128)(2,1)}) fusion(bf16[2,2,2048,128]{3,2,1,0:T(8,128)(2,1)} %bitcast.64, bf16[2,2,4096,128]{3,2,1,0:T(8,128)(2,1)} %bitcast.52), kind=kLoop, calls=%fused_computation.7 | loop fusion | flops 12582912 | bytes 12582912 | tf_op jit(solution)/shard_map/squeeze | solution.py:173
  107.8 51.4 %shard_map.136 = (bf16[2,128,16,128]{3,2,1,0:T(8,128)(2,1)}, bf16[2,128,16,128]{3,2,1,0:T(8,128)(2,1)}, bf16[2,6144,128]{2,1,0:T(8,128)(2,1)}, bf16[2,6144,128]{2,1,0:T(8,128)(2,1)}) custom-call(s32[8]{0:T(128)} %concatenate.6.meta, bf16[2,128,16,128]{3,2,1,0:T(8,128)(2,1)} %bitcast.59, bf16[2,128,16,128]{3,2,1,0:T(8,128)(2,1)} %bitcast.60, ...), custom_call_target="tpu_custom_call" | custom-call | tf_op jit(solution)/shard_map/pallas_call | solution.py:173
  159.3 2.5 copy.45
  161.8 4.5 %all-to-all-start.3 = ((bf16[2,128,16,128]{3,2,0,1:T(8,128)(2,1)}), bf16[2,128,16,128]{3,2,0,1:T(8,128)(2,1)}, u32[]{:S(2)}, u32[]{:S(2)}) async-start(bf16[2,128,16,128]{3,2,0,1:T(8,128)(2,1)} %copy.45), calls=%async_computation.3 | async-start | bytes 2097152 | tf_op jit(solution)/shard_map/all_to_all | solution.py:184
  169.2 10.9 %all-to-all-done.3 = bf16[2,128,16,128]{3,2,0,1:T(8,128)(2,1)} async-done(((bf16[2,128,16,128]{3,2,0,1:T(8,128)(2,1)}), bf16[2,128,16,128]{3,2,0,1:T(8,128)(2,1)}, u32[]{:S(2)}, u32[]{:S(2)}) %all-to-all-start.3) | async-done | bytes 1048608 | tf_op jit(solution)/shard_map/all_to_all | solution.py:184
  180.1 11.5 %all-to-all-start.5 = ((bf16[2,2,2,8,128,128]{5,4,2,1,0,3:T(8,128)(2,1)}), bf16[2,2,2,8,128,128]{5,4,2,1,0,3:T(8,128)(2,1)}, u32[]{:S(2)}, u32[]{:S(2)}) async-start(bf16[2,2,2,8,128,128]{5,4,2,1,0,3:T(8,128)(2,1)} %copy.49), calls=%async_computation.5 | async-start | bytes 4194304 | tf_op jit(solution)/shard_map/all_to_all | solution.py:176
  191.7 2.4 copy.47
  194.0 24.1 %all-to-all-done.5 = bf16[2,2,2,8,128,128]{5,4,2,1,0,3:T(8,128)(2,1)} async-done(((bf16[2,2,2,8,128,128]{5,4,2,1,0,3:T(8,128)(2,1)}), bf16[2,2,2,8,128,128]{5,4,2,1,0,3:T(8,128)(2,1)}, u32[]{:S(2)}, u32[]{:S(2)}) %all-to-all-start.5) | async-done | bytes 2097184 | tf_op jit(solution)/shard_map/all_to_all | solution.py:176
  218.1 4.4 %all-to-all-start.4 = ((bf16[2,128,16,128]{3,2,0,1:T(8,128)(2,1)}), bf16[2,128,16,128]{3,2,0,1:T(8,128)(2,1)}, u32[]{:S(2)}, u32[]{:S(2)}) async-start(bf16[2,128,16,128]{3,2,0,1:T(8,128)(2,1)} %copy.47), calls=%async_computation.4 | async-start | bytes 2097152 | tf_op jit(solution)/shard_map/all_to_all | solution.py:185
  225.5 11.4 %all-to-all-done.4 = bf16[2,128,16,128]{3,2,0,1:T(8,128)(2,1)} async-done(((bf16[2,128,16,128]{3,2,0,1:T(8,128)(2,1)}), bf16[2,128,16,128]{3,2,0,1:T(8,128)(2,1)}, u32[]{:S(2)}, u32[]{:S(2)}) %all-to-all-start.4) | async-done | bytes 1048608 | tf_op jit(solution)/shard_map/all_to_all | solution.py:185
  236.9 3.4 all-to-all-start.6
  242.5 3.4 copy.55
  245.9 21.2 %all-to-all-start.7 = ((bf16[2,2,2,64,32,128]{5,4,2,1,0,3:T(8,128)(2,1)}), bf16[2,2,2,64,32,128]{5,4,2,1,0,3:T(8,128)(2,1)}, u32[]{:S(2)}, u32[]{:S(2)}) async-start(bf16[2,2,2,64,32,128]{5,4,2,1,0,3:T(8,128)(2,1)} %copy.55), calls=%async_computation.7 | async-start | bytes 8388608 | tf_op jit(solution)/shard_map/all_to_all | solution.py:181
  267.0 2.4 copy.46
  273.4 45.4 %all-to-all-done.7 = bf16[2,2,2,64,32,128]{5,4,2,1,0,3:T(8,128)(2,1)} async-done(((bf16[2,2,2,64,32,128]{5,4,2,1,0,3:T(8,128)(2,1)}), bf16[2,2,2,64,32,128]{5,4,2,1,0,3:T(8,128)(2,1)}, u32[]{:S(2)}, u32[]{:S(2)}) %all-to-all-start.7) | async-done | bytes 4194336 | tf_op jit(solution)/shard_map/all_to_all | solution.py:181
  318.8 3.0 reduce_sum.25
  321.8 15.5 %all_gather.11 = bf16[2,2,2,256,128]{4,3,2,1,0:T(8,128)(2,1)S(1)} all-gather(bf16[2,2,2,32,128]{4,3,2,1,0:T(8,128)(2,1)S(1)} %reduce_sum.25), channel_id=1, replica_groups=mesh['prefix'=8,'resp'=8,'mp'=2] {'resp'}, dimensions={3}, use_global_device_ids=true | all-gather | bytes 589824 | tf_op jit(solution)/shard_map/all_gather | solution.py:183
  (46 shorter events, 23.4 us)
Async XLA Ops:
  7.2 75.1 %copy-start = (s32[2]{0:T(128)S(1)}, s32[2]{0:T(128)}, u32[]{:S(2)}) copy-start(s32[2]{0:T(128)} %param.16) | copy-start | bytes 28
  7.2 15.8 %copy-start.2 = (bf16[2,64,32,128]{3,2,1,0:T(8,128)(2,1)S(1)}, bf16[2,64,32,128]{3,2,1,0:T(8,128)(2,1)}, u32[]{:S(2)}) copy-start(bf16[2,64,32,128]{3,2,1,0:T(8,128)(2,1)} %param.9) | copy-start | bytes 3145732
  7.2 20.8 %copy-start.3 = (bf16[2,64,32,128]{3,2,1,0:T(8,128)(2,1)S(1)}, bf16[2,64,32,128]{3,2,1,0:T(8,128)(2,1)}, u32[]{:S(2)}) copy-start(bf16[2,64,32,128]{3,2,1,0:T(8,128)(2,1)} %param.14) | copy-start | bytes 3145732
  7.2 91.2 %all-gather.3.cloned.1.call-start = ((), (), s32[]{:S(2)}) async-start(), calls=%async_computation.8 | async-start | bytes 4718592 | tf_op jit(solution)/shard_map/all_gather | solution.py:166
  10.1 93.0 %all-gather.5.cloned.1.call-start = ((), (), s32[]{:S(2)}) async-start(), calls=%async_computation.9 | async-start | bytes 2359296 | tf_op jit(solution)/shard_map/all_gather | solution.py:164
  23.0 59.1 %copy-start.5 = (s32[16]{0:T(128)S(1)}, s32[16]{0:T(128)}, u32[]{:S(2)}) copy-start(s32[16]{0:T(128)} %param.17) | copy-start | bytes 196
  23.0 59.2 %copy-start.4 = (s32[16]{0:T(128)S(1)}, s32[16]{0:T(128)}, u32[]{:S(2)}) copy-start(s32[16]{0:T(128)} %param.15) | copy-start | bytes 196
  24.4 54.1 %all-to-all-start = ((bf16[2,64,32,128]{3,1,0,2:T(8,128)(2,1)}), bf16[2,64,32,128]{3,1,0,2:T(8,128)(2,1)S(1)}, u32[]{:S(2)}, u32[]{:S(2)}) async-start(bf16[2,64,32,128]{3,1,0,2:T(8,128)(2,1)} %copy.37), calls=%async_computation | async-start | bytes 2097152 | tf_op jit(solution)/shard_map/all_to_all | solution.py:160
  78.5 18.3 %all-to-all-start.1 = ((bf16[2,64,32,128]{3,1,0,2:T(8,128)(2,1)}), bf16[2,64,32,128]{3,1,0,2:T(8,128)(2,1)S(1)}, u32[]{:S(2)}, u32[]{:S(2)}) async-start(bf16[2,64,32,128]{3,1,0,2:T(8,128)(2,1)} %copy.39), calls=%async_computation.1 | async-start | bytes 2097152 | tf_op jit(solution)/shard_map/all_to_all | solution.py:161
  159.3 7.0 %copy-start.1 = (bf16[2,6144,128]{2,1,0:T(8,128)(2,1)S(1)}, bf16[2,6144,128]{2,1,0:T(8,128)(2,1)}, u32[]{:S(2)}) copy-start(bf16[2,6144,128]{2,1,0:T(8,128)(2,1)} %get-tuple-element.12) | copy-start | bytes 9437188
  161.8 18.3 %all-to-all-start.3 = ((bf16[2,128,16,128]{3,2,0,1:T(8,128)(2,1)}), bf16[2,128,16,128]{3,2,0,1:T(8,128)(2,1)}, u32[]{:S(2)}, u32[]{:S(2)}) async-start(bf16[2,128,16,128]{3,2,0,1:T(8,128)(2,1)} %copy.45), calls=%async_computation.3 | async-start | bytes 2097152 | tf_op jit(solution)/shard_map/all_to_all | solution.py:184
  180.1 38.0 %all-to-all-start.5 = ((bf16[2,2,2,8,128,128]{5,4,2,1,0,3:T(8,128)(2,1)}), bf16[2,2,2,8,128,128]{5,4,2,1,0,3:T(8,128)(2,1)}, u32[]{:S(2)}, u32[]{:S(2)}) async-start(bf16[2,2,2,8,128,128]{5,4,2,1,0,3:T(8,128)(2,1)} %copy.49), calls=%async_computation.5 | async-start | bytes 4194304 | tf_op jit(solution)/shard_map/all_to_all | solution.py:176
  218.1 18.8 %all-to-all-start.4 = ((bf16[2,128,16,128]{3,2,0,1:T(8,128)(2,1)}), bf16[2,128,16,128]{3,2,0,1:T(8,128)(2,1)}, u32[]{:S(2)}, u32[]{:S(2)}) async-start(bf16[2,128,16,128]{3,2,0,1:T(8,128)(2,1)} %copy.47), calls=%async_computation.4 | async-start | bytes 2097152 | tf_op jit(solution)/shard_map/all_to_all | solution.py:185
  236.9 9.0 %all-to-all-start.6 = ((bf16[2,2,128,2,128]{4,3,1,0,2:T(2,128)(2,1)}), bf16[2,2,128,2,128]{4,3,1,0,2:T(2,128)(2,1)S(1)}, u32[]{:S(2)}, u32[]{:S(2)}) async-start(bf16[2,2,128,2,128]{4,3,1,0,2:T(2,128)(2,1)} %copy.51), calls=%async_computation.6 | async-start | bytes 524288 | tf_op jit(solution)/shard_map/all_to_all | solution.py:179
  245.9 73.0 %all-to-all-start.7 = ((bf16[2,2,2,64,32,128]{5,4,2,1,0,3:T(8,128)(2,1)}), bf16[2,2,2,64,32,128]{5,4,2,1,0,3:T(8,128)(2,1)}, u32[]{:S(2)}, u32[]{:S(2)}) async-start(bf16[2,2,2,64,32,128]{5,4,2,1,0,3:T(8,128)(2,1)} %copy.55), calls=%async_computation.7 | async-start | bytes 8388608 | tf_op jit(solution)/shard_map/all_to_all | solution.py:181
Sparse Core Ops, SparseCore 0:
  10.2 55.9 all-gather.2
  68.4 24.1 all-gather.4

commit v2 on v1

--- a/solution.py
+++ b/solution.py
@@ -14,7 +14,7 @@
 
 def attend(KB=256, RC=256, variant="wt"):
     C2=math.log2(math.e)/math.sqrt(HD); INV=1/math.sqrt(HD)
-    def kernel(meta, q_ref, c_ref, k_ref, v_ref, o_ref, dq_ref, dk_ref, dv_ref,
+    def kernel(meta, q_ref, c_ref, kv_ref, o_ref, dq_ref, dkv_ref,
                qhl, qr, dr, S, Pm, mx, ls, oacc, dqacc, dkacc, dvacc, ocat, dqcat):
         pos0=meta[0]
         dkacc[...]=jnp.zeros_like(dkacc); dvacc[...]=jnp.zeros_like(dvacc)
@@ -49,7 +49,7 @@
             oacc[...]=jnp.zeros_like(oacc)
             def passA(i,_):
                 isp,j,row=place(i)
-                kb=k_ref[h,pl.ds(row,KB)]
+                kb=kv_ref[0,h,pl.ds(row,KB)]
                 kk=jnp.concatenate([kb,kb],axis=1)
                 col=lax.broadcasted_iota(jnp.int32,(RC,KB),1)
                 base=jnp.where(isp,i*KB,j*KB)
@@ -69,7 +69,7 @@
                 mx[pl.ds(rc,RC)]=jnp.broadcast_to(m,(RC,128))
             def passB(i,_):
                 isp,j,row=place(i)
-                vb=v_ref[h,pl.ds(row,KB)]
+                vb=kv_ref[1,h,pl.ds(row,KB)]
                 for rc in range(0,R,RC):
                     m=mx[pl.ds(rc,RC)]
                     s=S[pl.ds(rc,RC),pl.ds(pl.multiple_of(i*KB,KB),KB)]
@@ -102,8 +102,8 @@
             dqacc[...]=jnp.zeros_like(dqacc)
             def passC(i,_):
                 isp,j,row=place(i)
-                vb=v_ref[h,pl.ds(row,KB)]
-                kb=k_ref[h,pl.ds(row,KB)]
+                vb=kv_ref[1,h,pl.ds(row,KB)]
+                kb=kv_ref[0,h,pl.ds(row,KB)]
                 dss=[]
                 cs=pl.ds(pl.multiple_of(i*KB,KB),KB)
                 for rc in range(0,R,RC):
@@ -138,8 +138,8 @@
         def finkv(i,_):
             for h in range(2):
                 rows=pl.ds(pl.multiple_of(i*512,512),512)
-                dk_ref[h,rows]=(dkacc[h,rows]*INV).astype(jnp.bfloat16)
-                dv_ref[h,rows]=dvacc[h,rows].astype(jnp.bfloat16)
+                dkv_ref[0,h,rows]=(dkacc[h,rows]*INV).astype(jnp.bfloat16)
+                dkv_ref[1,h,rows]=dvacc[h,rows].astype(jnp.bfloat16)
             return 0
         lax.fori_loop(0,ROWS//512,finkv,0)
     bf=jnp.bfloat16; f32=jnp.float32
@@ -150,40 +150,233 @@
              pltpu.VMEM((2,2,R,HD),f32),pltpu.VMEM((2,2,R,HD),f32)]
     return pl.pallas_call(kernel,
         out_shape=[jax.ShapeDtypeStruct((2,T,16,HD),bf),jax.ShapeDtypeStruct((2,T,16,HD),bf),
-                   jax.ShapeDtypeStruct((2,ROWS,HD),bf),jax.ShapeDtypeStruct((2,ROWS,HD),bf)],
-        in_specs=[pl.BlockSpec(memory_space=pltpu.SMEM),V,V,V,V],out_specs=[V]*4,
+                   jax.ShapeDtypeStruct((2,2,ROWS,HD),bf)],
+        in_specs=[pl.BlockSpec(memory_space=pltpu.SMEM),V,V,V],out_specs=[V]*3,
         scratch_shapes=scratch,
         compiler_params=pltpu.CompilerParams(vmem_limit_bytes=60*2**20))
 
 
+MESH = pl.DeviceIdType.MESH
+HBM = pl.BlockSpec(memory_space=pl.ANY)
+VM = pl.BlockSpec(memory_space=pltpu.VMEM)
+BF = jnp.bfloat16
+F32 = jnp.float32
+
+
+class Mover:
+    def __init__(self, send, recv, local):
+        self.send, self.recv, self.local, self.n, self.m = send, recv, local, 0, 0
+        self.remote, self.near = [], []
+
+    def to(self, src, dst, where):
+        cp = pltpu.make_async_remote_copy(
+            src_ref=src, dst_ref=dst, send_sem=self.send.at[self.n], recv_sem=self.recv.at[self.n],
+            device_id=where, device_id_type=MESH)
+        self.n += 1
+        cp.start()
+        self.remote.append(cp)
+        return cp
+
+    def here(self, src, dst):
+        cp = pltpu.make_async_copy(src, dst, self.local.at[self.m])
+        self.m += 1
+        cp.start()
+        return cp
+
+    def drain(self):
+        for cp in self.remote:
+            cp.wait_send()
+
+
+def place_of():
+    p, r, m = lax.axis_index("prefix"), lax.axis_index("resp"), lax.axis_index("mp")
+    zl, y, x, c = p // 4, p % 4, r // 2, r % 2
+    sib = {"resp": x * 2 + 1 - c}
+    mate = {"mp": 1 - m}
+    zmate = {"prefix": (1 - zl) * 4 + y}
+    xs = [{"resp": ((x + d) % 4) * 2 + c} for d in (1, 2, 3)]
+    ys = [{"prefix": zl * 4 + (y + d) % 4} for d in (1, 2, 3)]
+    return zl, y, x, c, m, sib, mate, zmate, xs, ys
+
+
+def meet(peers):
+    barrier = pltpu.get_barrier_semaphore()
+    for peer in peers:
+        pl.semaphore_signal(barrier, inc=1, device_id=peer, device_id_type=MESH)
+    pl.semaphore_wait(barrier, len(peers))
+
+
+def bring_kernel(q, g, rkv, pkv, qh, gh, kv, send, recv, local):
+    zl, y, x, c, m, sib, mate, zmate, xs, ys = place_of()
+    mv = Mover(send, recv, local)
+    own = []
+    T2 = T // 2
+    mine_r = x * 256 + c * 128
+    own.append(mv.here(rkv.at[:, pl.ds(2 * m, 2)], kv.at[:, :, 2, :, pl.ds(mine_r + m * T2, T2)]))
+    for a in range(2):
+        own.append(mv.here(pkv.at[a], kv.at[a, :, 0:2, zl, pl.ds(y * 256, 256)]))
+    meet([sib, mate, zmate] + xs + ys)
+    b1 = mv.to(rkv.at[:, pl.ds(2 * (1 - m), 2)], kv.at[:, :, 2, :, pl.ds(mine_r + m * T2, T2)], mate)
+    c1 = mv.to(pkv.at[c], kv.at[c, :, 0:2, zl, pl.ds(y * 256, 256)], zmate)
+    c2a = [mv.to(pkv.at[c], kv.at[c, :, 0:2, zl, pl.ds(y * 256, 256)], w) for w in ys]
+    swaps = []
+    for b in range(2):
+        for s, d in ((q, qh), (g, gh)):
+            swaps.append(mv.to(s.at[b, :, pl.ds(16 * (1 - m), 16)], d.at[b, pl.ds(T2 * m, T2)], mate))
+            own.append(mv.here(s.at[b, :, pl.ds(16 * m, 16)], d.at[b, pl.ds(T2 * m, T2)]))
+    own[0].wait()
+    b1.wait_recv()
+    rblk = lambda xx: kv.at[:, :, 2, :, pl.ds(xx * 256 + c * 128, 128)]
+    b2 = [mv.to(rblk(x), rblk(x), w) for w in xs]
+    b3 = [mv.to(rblk(x), rblk(x), sib)]
+    pblk = lambda z, yy: kv.at[c, :, 0:2, z, pl.ds(yy * 256, 256)]
+    c1.wait_recv()
+    c2b = [mv.to(pblk(1 - zl, y), pblk(1 - zl, y), w) for w in ys]
+    c3 = [mv.to(pblk(1 - zl, y), pblk(1 - zl, y), sib)]
+    for d in (0, 2, 1):
+        yy, xx = (y + 3 - d) % 4, (x + 3 - d) % 4
+        c2a[d].wait_recv()
+        c3.append(mv.to(pblk(zl, yy), pblk(zl, yy), sib))
+        b2[d].wait_recv()
+        b3.append(mv.to(rblk(xx), rblk(xx), sib))
+    for d in (0, 2, 1):
+        yy = (y + 3 - d) % 4
+        c2b[d].wait_recv()
+        c3.append(mv.to(pblk(1 - zl, yy), pblk(1 - zl, yy), sib))
+    for cp in b3 + c3 + swaps:
+        cp.wait_recv()
+    for cp in own[1:]:
+        cp.wait()
+    mv.drain()
+
+
+def bring(q, g, rkv, pkv):
+    return pl.pallas_call(
+        bring_kernel,
+        out_shape=[jax.ShapeDtypeStruct((2, T, 16, HD), BF)] * 2 + [jax.ShapeDtypeStruct((2, 2, 3, 2, 1024, HD), BF)],
+        in_specs=[HBM] * 4,
+        out_specs=[HBM] * 3,
+        scratch_shapes=[pltpu.SemaphoreType.DMA((32,)), pltpu.SemaphoreType.DMA((32,)), pltpu.SemaphoreType.DMA((8,))],
+        compiler_params=pltpu.CompilerParams(collective_id=1, has_side_effects=True),
+    )(q, g, rkv, pkv)
+
+
+def share_kernel(o, dq, terms, out, dout, fin, fr, far, s0, r1, s1, r2, s2, r3, rr1, rs, send, recv, local):
+    zl, y, x, c, m, sib, mate, zmate, xs, ys = place_of()
+    mv = Mover(send, recv, local)
+    T2 = T // 2
+    meet([sib, mate, zmate] + xs + ys)
+    first = [mv.to(terms.at[1 - c, h], far.at[h], sib) for h in range(2)]
+    own, swaps = [], []
+    for b in range(2):
+        for s, d in ((o, out), (dq, dout)):
+            swaps.append(mv.to(s.at[b, pl.ds(T2 * (1 - m), T2)], d.at[b, :, pl.ds(16 * m, 16)], mate))
+            own.append(mv.here(s.at[b, pl.ds(T2 * m, T2)], d.at[b, :, pl.ds(16 * m, 16)]))
+    sent1, sentr = [], []
+    for h in range(2):
+        first[h].wait_recv()
+        for i in range(3):
+            for j in range(2):
+                for k in range(4):
+                    s0[h, i, j, k] = (terms[c, h, i, j, k].astype(F32) + far[h, i, j, k].astype(F32)).astype(BF)
+        for d in range(3):
+            if h == 0:
+                part = s0.at[h, 0:2, :, :, (x + 1 + d) % 4]
+            else:
+                part = s0.at[h, 0:2, :, (y + 1 + d) % 4]
+            sent1.append(mv.to(part, r1.at[h, d], xs[d] if h == 0 else ys[d]))
+        for d in range(3):
+            sentr.append(mv.to(s0.at[h, 2, :, (x + 1 + d) % 4], rr1.at[h, d], xs[d]))
+    sent2 = []
+    for h in range(2):
+        for d in range(3):
+            sent1[3 * h + d].wait_recv()
+        for i in range(2):
+            for j in range(2):
+                for k in range(4):
+                    a = s0[h, i, j, k, x] if h == 0 else s0[h, i, j, y, k]
+                    t = a.astype(F32)
+                    for d in range(3):
+                        t = t + r1[h, d, i, j, k].astype(F32)
+                    s1[h, i, j, k] = t.astype(BF)
+        for d in range(3):
+            at = (y if h == 0 else x) + 1 + d
+            sent2.append(mv.to(s1.at[h, :, :, at % 4], r2.at[h, d], ys[d] if h == 0 else xs[d]))
+    for d in range(6):
+        sentr[d].wait_recv()
+    for h in range(2):
+        for b in range(2):
+            for k in range(4):
+                t = s0[h, 2, b, x, k].astype(F32)
+                for d in range(3):
+                    t = t + rr1[h, d, b, k].astype(F32)
+                rs[c, h, b, k] = t.astype(BF)
+    pair = mv.to(rs.at[c, :, :, pl.ds(2 * (1 - c), 2)], rs.at[c, :, :, pl.ds(2 * (1 - c), 2)], sib)
+    sent3 = []
+    for h in range(2):
+        for d in range(3):
+            sent2[3 * h + d].wait_recv()
+        for i in range(2):
+            for j in range(2):
+                t = s1[h, i, j, y if h == 0 else x].astype(F32)
+                for d in range(3):
+                    t = t + r2[h, d, i, j].astype(F32)
+                s2[h, i, j] = t.astype(BF)
+        sent3.append(mv.to(s2.at[h, :, 1 - zl], r3.at[h], zmate))
+    pair.wait_recv()
+    mine = mv.here(rs.at[:, :, :, 2 * c + m], fr.at[:, pl.ds(2 * m, 2)])
+    last = mv.to(rs.at[:, :, :, 2 * c + 1 - m], fr.at[:, pl.ds(2 * m, 2)], mate)
+    for h in range(2):
+        sent3[h].wait_recv()
+        for i in range(2):
+            fin[c, h, i, x] = (s2[h, i, zl].astype(F32) + r3[h, i].astype(F32)).astype(BF)
+    spread = [mv.to(fin.at[c, :, :, x], fin.at[c, :, :, x], w) for w in xs]
+    twin = [mv.to(fin.at[c, :, :, x], fin.at[c, :, :, x], sib)]
+    for d in (0, 2, 1):
+        spread[d].wait_recv()
+        xx = (x + 3 - d) % 4
+        twin.append(mv.to(fin.at[c, :, :, xx], fin.at[c, :, :, xx], sib))
+    for cp in twin + swaps + [last]:
+        cp.wait_recv()
+    for cp in own + [mine]:
+        cp.wait()
+    mv.drain()
+
+
+def share(o, dq, terms):
+    v = pltpu.VMEM
+    return pl.pallas_call(
+        share_kernel,
+        out_shape=[jax.ShapeDtypeStruct((2, T // 2, 32, HD), BF)] * 2
+        + [jax.ShapeDtypeStruct((2, 2, 2, 4, 64, HD), BF), jax.ShapeDtypeStruct((2, 4, 2, 64, HD), BF)],
+        in_specs=[HBM, HBM, VM],
+        out_specs=[HBM, HBM, VM, VM],
+        scratch_shapes=[
+            v((2, 3, 2, 4, 4, 64, HD), BF), v((2, 3, 2, 4, 4, 64, HD), BF),
+            v((2, 3, 2, 2, 4, 64, HD), BF), v((2, 2, 2, 4, 64, HD), BF),
+            v((2, 3, 2, 2, 64, HD), BF), v((2, 2, 2, 64, HD), BF), v((2, 2, 64, HD), BF),
+            v((2, 3, 2, 4, 64, HD), BF), v((2, 2, 2, 4, 64, HD), BF),
+            pltpu.SemaphoreType.DMA((40,)), pltpu.SemaphoreType.DMA((40,)), pltpu.SemaphoreType.DMA((8,)),
+        ],
+        compiler_params=pltpu.CompilerParams(collective_id=2, has_side_effects=True, vmem_limit_bytes=48 * 2**20),
+    )(o, dq, terms)
+
+
 def per_device(queries, resp_keys, resp_values, prefix_keys, prefix_values, grad_out, prompt_ids, prefix_lengths, resp_lengths):
-    q = lax.all_to_all(queries, "mp", split_axis=2, concat_axis=1, tiled=True)
-    c = lax.all_to_all(grad_out, "mp", split_axis=2, concat_axis=1, tiled=True)
-    kv = jnp.stack([resp_keys, resp_values])
-    kv = lax.all_to_all(kv, "mp", split_axis=3, concat_axis=2, tiled=True)
-    kv = lax.all_gather(kv.transpose(0, 3, 1, 2, 4), "resp", axis=3, tiled=True)
-    pre = jnp.stack([prefix_keys, prefix_values]).transpose(0, 3, 1, 2, 4)
-    pre = lax.all_gather(pre, "prefix", axis=3, tiled=True)
-    flat = jnp.concatenate([pre.reshape(2, 2, 2 * PRE, HD), kv.reshape(2, 2, 2 * RL, HD)], axis=2)
+    rkv = jnp.stack([resp_keys, resp_values]).transpose(0, 3, 1, 2, 4)
+    pkv = jnp.stack([prefix_keys, prefix_values]).transpose(0, 3, 1, 2, 4)
+    q, g, kv = bring(queries, grad_out, rkv, pkv)
+    kv = kv.reshape(2, 2, ROWS, HD)
     first = lax.axis_index("prefix") * 2
     prompts = lax.dynamic_slice_in_dim(prompt_ids, first, 2)
     lengths = lax.dynamic_slice_in_dim(resp_lengths, first, 2)
     pos0 = lax.axis_index("resp") * T
     meta = jnp.concatenate([pos0[None], prompts, lengths, prefix_lengths[prompts], jnp.zeros((1,), jnp.int32)]).astype(jnp.int32)
-    o, dq, dk, dv = attend()(meta, q, c, flat[0], flat[1])
-    terms = jnp.stack([dk, dv])
-    rt = terms[:, :, 2 * PRE :].reshape(2, 2, 2, 8, T, HD)
-    rt = lax.all_to_all(rt, "resp", split_axis=3, concat_axis=3, tiled=True)
-    rt = jnp.sum(rt.astype(jnp.float32), axis=3).astype(jnp.bfloat16)
-    rt = rt.transpose(0, 2, 3, 1, 4)
-    rt = lax.all_to_all(rt, "mp", split_axis=2, concat_axis=3, tiled=True)
-    pt = terms[:, :, : 2 * PRE].reshape(2, 2, 2, 64, 32, HD)
-    pt = lax.all_to_all(pt, ("prefix", "resp"), split_axis=3, concat_axis=3, tiled=True)
-    pt = jnp.sum(pt.astype(jnp.float32), axis=3).astype(jnp.bfloat16)
-    pt = lax.all_gather(pt, "resp", axis=3, tiled=True).transpose(0, 2, 3, 1, 4)
-    attention = lax.all_to_all(o, "mp", split_axis=1, concat_axis=2, tiled=True)
-    d_queries = lax.all_to_all(dq, "mp", split_axis=1, concat_axis=2, tiled=True)
-    return (attention, d_queries, rt[0], rt[1], pt[0], pt[1])
+    o, dq, terms = attend()(meta, q, g, kv)
+    attention, d_queries, fin, fr = share(o, dq, terms.reshape(2, 2, 3, 2, 4, 4, 64, HD))
+    fin = fin.reshape(2, 2, 2, 256, HD).transpose(0, 2, 3, 1, 4)
+    fr = fr.transpose(0, 2, 3, 1, 4)
+    return (attention, d_queries, fr[0], fr[1], fin[0], fin[1])
 
 
 def solution(mesh):

time: 347 us -> 192 us (0.55)
  waiting for transfers between devices: 153 us -> 0 us
  Pallas kernels: 51.4 us -> 177 us
  starting transfers between devices: 52.3 us -> 0 us
  blocking collectives: 26.6 us -> 0 us
  local copies, waits for them, and re-layouts: 32.8 us -> 11.7 us
  other arithmetic: 16.3 us -> 2.31 us
  between operations: 14.2 us -> 0.69 us
    all_to_all x7 -> x0, waiting for transfers between devices: 153 us -> none  [the longest x1 49.2 us: per_device(): q = lax.all_to_all(queries, 'mp', split_axis=2, concat_axis=1, tiled=True)]
    pallas_call x1 -> x3, Pallas kernels: 51.4 us -> 177 us  [the longest x1 69.7 us: per_device(): o, dq, terms = attend()(meta, q, g, kv)]
    all_to_all x7 -> x0, starting transfers between devices: 52.2 us -> none  [the longest x1 21.2 us: per_device(): lax.all_to_all(pt, ('prefix', 'resp'), split_axis=3, concat_axis=3, tiled...]
    all_gather x1 -> x0, blocking collectives: 15.5 us -> none  [per_device(): pt = lax.all_gather(pt, 'resp', axis=3, tiled=True).transpose(0, 2, 3, 1, 4)]
    all_to_all x1 -> x0, blocking collectives: 11 us -> none  [per_device(): kv = lax.all_to_all(kv, 'mp', split_axis=3, concat_axis=2, tiled=True)]
    all_to_all x6 -> x0, local copies, waits for them, and re-layouts: 8.8 us -> none  [the longest x1 2.37 us: per_device(): attention = lax.all_to_all(o, 'mp', split_axis=1, concat_axis=2, tiled=True)]
    reduce_sum x2 -> x0, other arithmetic: 4.99 us -> none  [the longest x1 3.02 us: per_device(): pt = jnp.sum(pt.astype(jnp.float32), axis=3).astype(jnp.bfloat16)]
    pallas_call x2 -> x0, local copies, waits for them, and re-layouts: 4.9 us -> none  [per_device(): o, dq, dk, dv = attend()(meta, q, c, flat[0], flat[1])]
  transfers between devices with their start and end apart: 9 -> 0, of which waited for: 6 -> 0; matrix products, arithmetic and copies ran while one was open for 10% -> 0% of each run, Pallas kernels for 0% -> 0%
where the time goes in v2:
time: 192 us; the launch traced here: 191 us
  Pallas kernels  177 us (92%)
  local copies, waits for them, and re-layouts  11.7 us (6%)
  other arithmetic  2.31 us (1%)
    pallas_call x1, Pallas kernels, per_device(): o, dq, terms = attend()(meta, q, g, kv)  69.7 us
    pallas_call x1, Pallas kernels, share(): pl.pallas_call(share_kernel, out_shape=[jax.ShapeDtypeStruct((2, T // 2,...  53.5 us
    pallas_call x1, Pallas kernels, bring(): pl.pallas_call(bring_kernel, out_shape=[jax.ShapeDtypeStruct((2, T, 16, H...  53.4 us
    unnamed x10, local copies, waits for them, and re-layouts  5.91 us

profile of v2, /device:TPU:1, one launch (start us, length us, event | category | flops | bytes accessed | tf_op | source)
XLA Modules:
  0.0 191.2 jit_solution(6552101272379126329)
XLA Ops:
  0.6 0.0 copy-start
  0.7 0.7 dynamic_slice.7
  1.4 0.7 compare_select_fusion
  2.1 0.0 copy-done
  2.1 0.6 gather_fusion
  2.8 0.6 concatenate.3.meta
  3.4 1.0 copy_bitcast_fusion.3
  4.4 0.7 maximum_bitcast_fusion.1.rkv
  5.1 1.1 copy_bitcast_fusion.1
  6.2 0.8 maximum_bitcast_fusion.pkv
  7.1 53.4 %shard_map.136 = (bf16[2,128,16,128]{3,2,1,0:T(8,128)(2,1)}, bf16[2,128,16,128]{3,2,1,0:T(8,128)(2,1)}, bf16[2,2,3,2,1024,128]{5,4,3,2,1,0:T(8,128)(2,1)}) custom-call(bf16[2,64,32,128]{3,2,1,0:T(8,128)(2,1)} %q.1, bf16[2,64,32,128]{3,2,1,0:T(8,128)(2,1)} %g.1, bf16[2,4,2,64,128]{4,3,2,1,0:T(8,128)(2,1)} %maximum_bitcast_fusion.1.rkv, ...), custom_call_target="tpu_custom_call" | custom-call | tf_op jit(solution)/shard_map/pallas_call | solution.py:254
  60.5 69.7 %shard_map.137 = (bf16[2,128,16,128]{3,2,1,0:T(8,128)(2,1)}, bf16[2,128,16,128]{3,2,1,0:T(8,128)(2,1)}, bf16[2,2,6144,128]{3,2,1,0:T(8,128)(2,1)}) custom-call(s32[8]{0:T(128)} %concatenate.3.meta, bf16[2,128,16,128]{3,2,1,0:T(8,128)(2,1)} %get-tuple-element.16.q_ref, bf16[2,128,16,128]{3,2,1,0:T(8,128)(2,1)} %get-tuple-element.17.c_ref, ...), custom_call_target="tpu_custom_call" | custom-call | tf_op jit(solution)/shard_map/pallas_call | solution.py:375
  130.1 0.0 copy-start.1
  130.1 1.2 copy-done.1
  131.3 0.0 copy-start.2
  131.3 1.2 copy-done.2
  132.6 53.5 %shard_map.138 = (bf16[2,64,32,128]{3,2,1,0:T(8,128)(2,1)S(1)}, bf16[2,64,32,128]{3,2,1,0:T(8,128)(2,1)S(1)}, bf16[2,2,2,4,64,128]{5,4,3,2,1,0:T(8,128)(2,1)S(1)}, bf16[2,4,2,64,128]{4,3,2,1,0:T(8,128)(2,1)S(1)}) custom-call(bf16[2,128,16,128]{3,2,1,0:T(8,128)(2,1)S(1)} %copy-done.1, bf16[2,128,16,128]{3,2,1,0:T(8,128)(2,1)S(1)} %copy-done.2, ...), custom_call_target="tpu_custom_call" | custom-call | tf_op jit(solution)/shard_map/pallas_call | solution.py:348
  186.1 0.8 copy.28
  186.8 0.8 copy.27
  187.6 0.5 copy.34
  188.2 1.2 slice_bitcast_fusion
  189.3 1.0 copy.37
  190.3 1.0 copy.38
  (2 shorter events, 0.0 us)
Async XLA Ops:
  0.6 1.5 copy-start
  130.1 1.2 copy-start.1
  131.3 1.2 copy-start.2

commit v3 on v1

v3 whole, which is shorter than its diff:
```python
import math

import jax
import jax.numpy as jnp
from jax import lax
from jax.experimental import pallas as pl
from jax.experimental.pallas import tpu as pltpu
from jax.sharding import PartitionSpec as P

HD = 128
PRE = 2048
RL = 1024
T = 128
T2 = T // 2
G = 8
R = T * G
KB = 1024
RC = 256
NT = (((1,), (1,)), ((), ()))
NN = (((1,), (0,)), ((), ()))
TN = (((0,), (0,)), ((), ()))
MESH = pl.DeviceIdType.MESH
HBM = pl.BlockSpec(memory_space=pl.ANY)
VM = pl.BlockSpec(memory_space=pltpu.VMEM)
SM = pl.BlockSpec(memory_space=pltpu.SMEM)
BF = jnp.bfloat16
F32 = jnp.float32
INV = 1.0 / math.sqrt(HD)
C2 = math.log2(math.e) / math.sqrt(HD)


def dot(a, b, dims):
    return lax.dot_general(a, b, dims, preferred_element_type=F32)


class Mover:
    def __init__(self, send, recv, local):
        self.send, self.recv, self.local, self.n, self.m = send, recv, local, 0, 0
        self.remote = []

    def to(self, src, dst, where):
        cp = pltpu.make_async_remote_copy(
            src_ref=src, dst_ref=dst, send_sem=self.send.at[self.n], recv_sem=self.recv.at[self.n],
            device_id=where, device_id_type=MESH)
        self.n += 1
        cp.start()
        self.remote.append(cp)
        return cp

    def here(self, src, dst):
        cp = pltpu.make_async_copy(src, dst, self.local.at[self.m])
        self.m += 1
        cp.start()
        return cp

    def drain(self):
        for cp in self.remote:
            cp.wait_send()


def got(copies):
    for cp in copies:
        cp.wait_recv()


def kernel(pid, plen_ref, rlen_ref, q, g, rkv, pkv, out, dout, fin, fr,
           qb, gb, pk0, pv0, pre1, res, S, Pm, D, qhl, qr, dr, mx, ls, oacc, dqacc, X, oh, dqh, ob, dqb,
           tm, far, s0, r1, s1, r2, s2, r3, rr1, rs, send, recv, local):
    p, r, m = lax.axis_index("prefix"), lax.axis_index("resp"), lax.axis_index("mp")
    zl, y, x, c = p // 4, p % 4, r // 2, r % 2
    sib = {"resp": x * 2 + 1 - c}
    mate = {"mp": 1 - m}
    zmate = {"prefix": (1 - zl) * 4 + y}
    xs = [{"resp": ((x + d) % 4) * 2 + c} for d in (1, 2, 3)]
    ys = [{"prefix": zl * 4 + (y + d) % 4} for d in (1, 2, 3)]
    mv = Mover(send, recv, local)
    pos0 = r * T
    mine_r = r * T
    half = c * 128

    own_q = [[mv.here(s.at[b, :, pl.ds(16 * m, 16)], d.at[b, pl.ds(T2 * m, T2)]) for s, d in ((q, qb), (g, gb))] for b in range(2)]
    own_r = mv.here(rkv.at[:, pl.ds(2 * m, 2)], res.at[:, :, :, pl.ds(mine_r + m * T2, T2)])
    own_p = [mv.here(pkv.at[0, 0], pk0.at[:, zl, pl.ds(y * 256, 256)]), mv.here(pkv.at[1, 0], pv0.at[:, zl, pl.ds(y * 256, 256)]),
             mv.here(pkv.at[:, 1], pre1.at[:, :, zl, pl.ds(y * 256, 256)])]
    peers = [sib, mate, zmate] + xs + ys
    barrier = pltpu.get_barrier_semaphore()
    for peer in peers:
        pl.semaphore_signal(barrier, inc=1, device_id=peer, device_id_type=MESH)
    pl.semaphore_wait(barrier, len(peers))

    pk_at = lambda z, yy: pk0.at[:, z, pl.ds(yy * 256 + half, 128)]
    pv_at = lambda z, yy: pv0.at[:, z, pl.ds(yy * 256 + half, 128)]
    p1_at = lambda z, yy: pre1.at[:, :, z, pl.ds(yy * 256 + half, 128)]
    r_at = lambda h, xx: res.at[:, h, :, pl.ds(xx * 256 + c * 128, 128)]

    def swap_in(b, s, d):
        return mv.to(s.at[b, :, pl.ds(16 * (1 - m), 16)], d.at[b, pl.ds(T2 * m, T2)], mate)

    def spread_z(src, at):
        return mv.to(src, at(zl, y), zmate), [mv.to(src, at(zl, y), w) for w in ys]

    def pass_z(cp, at):
        cp.wait_recv()
        return [mv.to(at(1 - zl, y), at(1 - zl, y), w) for w in ys], [mv.to(at(1 - zl, y), at(1 - zl, y), sib)]

    def pass_y(near, other, at):
        sent = []
        for z, cps in ((zl, near), (1 - zl, other)):
            for d in (0, 2, 1):
                yy = (y + 3 - d) % 4
                cps[d].wait_recv()
                sent.append(mv.to(at(z, yy), at(z, yy), sib))
        return sent

    def spread_r(h):
        return [mv.to(r_at(h, x), r_at(h, x), w) for w in xs], [mv.to(r_at(h, x), r_at(h, x), sib)]

    def pass_r(cps):
        sent = []
        for d in (0, 2, 1):
            xx = (x + 3 - d) % 4
            cps[0][d].wait_recv()
            sent.append(mv.to(cps[2](xx), cps[2](xx), sib))
        return sent

    mine_p = lambda kv, h: pkv.at[kv, h, :, pl.ds(half, 128)]
    rz = mv.to(rkv.at[:, pl.ds(2 * (1 - m), 2)], res.at[:, :, :, pl.ds(mine_r + m * T2, T2)], mate)
    kz, ky = spread_z(mine_p(0, 0), pk_at)
    q_in = [swap_in(0, q, qb), None]
    vz, vy = spread_z(mine_p(1, 0), pv_at)
    g_in = [swap_in(0, g, gb), None]
    own_r.wait()
    rz.wait_recv()
    rx0, rs0 = spread_r(0)
    ky2, ks = pass_z(kz, pk_at)
    vy2, vs = pass_z(vz, pv_at)
    ks += pass_y(ky, ky2, pk_at)
    rs0 += pass_r((rx0, None, lambda xx: r_at(0, xx)))
    for cp in own_q[0] + own_p:
        cp.wait()
    got([q_in[0]] + rs0 + ks)

    def prefix_rows(h, kv, prompt, i):
        if h == 0:
            ref = pk0 if kv == 0 else pv0
            return ref[prompt, i]
        return pre1[kv, prompt, i]

    def limits(b, rc, resp):
        if not resp:
            return plen_ref[pid[2 * p + b]] - 1
        t = pos0 + rc // G + lax.broadcasted_iota(jnp.int32, (RC, 1), 0) // G
        return jnp.minimum(t, rlen_ref[2 * p + b] - 1)

    def head_rows(ref, b, h, rc):
        a = ref[b, pl.ds(rc // G, RC // G)].astype(F32)
        return a[:, h * G : (h + 1) * G].reshape(RC, HD)

    def pass_a(h, b):
        prompt = pid[2 * p + b]
        for rc in range(0, R, RC):
            rows = pl.ds(rc, RC)
            a = head_rows(qb, b, h, rc)
            qr[rows] = a.astype(BF)
            a = a * C2
            hi = a.astype(BF)
            qhl[rows, 0:HD] = hi
            qhl[rows, HD : 2 * HD] = (a - hi.astype(F32)).astype(BF)
        mx[...] = jnp.full_like(mx, -jnp.inf)

        def block(kb, col0, base, resp):
            kk = jnp.concatenate([kb, kb], axis=1)
            col = base + lax.broadcasted_iota(jnp.int32, (RC, KB), 1)
            for rc in range(0, R, RC):
                rows = pl.ds(rc, RC)
                s = dot(qhl[rows], kk, NT)
                s = jnp.where(col <= limits(b, rc, resp), s, -1e30)
                S[rows, pl.ds(col0, KB)] = s
                top = mx[rows]
                for k in range(0, KB, 128):
                    top = jnp.maximum(top, s[:, k : k + 128])
                mx[rows] = top

        def step(i, _):
            start = pl.multiple_of(i * KB, KB)
            block(prefix_rows(h, 0, prompt, i), start, start, False)
            return 0

        lax.fori_loop(0, PRE // KB, step, 0)
        block(res[0, h, b], PRE, 0, True)
        for rc in range(0, R, RC):
            rows = pl.ds(rc, RC)
            mx[rows] = jnp.broadcast_to(jnp.max(mx[rows], axis=1, keepdims=True), (RC, 128))

    def pass_b(h, b):
        prompt = pid[2 * p + b]
        ls[...] = jnp.zeros_like(ls)
        oacc[...] = jnp.zeros_like(oacc)

        def block(vb, col0):
            cols = pl.ds(col0, KB)
            for rc in range(0, R, RC):
                rows = pl.ds(rc, RC)
                top = mx[rows]
                s = S[rows, cols]
                total = ls[rows]
                parts = []
                for k in range(0, KB, 128):
                    e = jnp.exp2(s[:, k : k + 128] - top)
                    total = total + e
                    parts.append(e.astype(BF))
                ls[rows] = total
                pb = jnp.concatenate(parts, axis=1)
                Pm[rows, cols] = pb
                oacc[rows] += dot(pb, vb, NN)

        def step(i, _):
            block(prefix_rows(h, 1, prompt, i), pl.multiple_of(i * KB, KB))
            return 0

        lax.fori_loop(0, PRE // KB, step, 0)
        block(res[1, h, b], PRE)
        for rc in range(0, R, RC):
            rows = pl.ds(rc, RC)
            il = 1.0 / jnp.sum(ls[rows], axis=1, keepdims=True)
            o = (oacc[rows] * il).astype(BF).astype(F32)
            if h == 0:
                oh[b, rows] = o
            else:
                both = jnp.concatenate([oh[b, rows].reshape(RC // G, G, HD), o.reshape(RC // G, G, HD)], axis=1)
                ob[b, pl.ds(rc // G, RC // G)] = both.astype(BF)
            d = head_rows(gb, b, h, rc)
            t = pos0 + rc // G + lax.broadcasted_iota(jnp.int32, (RC, 1), 0) // G
            d = jnp.where(t < rlen_ref[2 * p + b], d, 0.0)
            delta = jnp.sum(d * o, axis=1, keepdims=True)
            dr[rows] = (d * il).astype(BF)
            mx[rows] = jnp.broadcast_to(delta * il, (RC, 128))

    def pass_c(h, b):
        prompt = pid[2 * p + b]
        dqacc[...] = jnp.zeros_like(dqacc)

        def block(kb, vb, col0):
            cols = pl.ds(col0, KB)
            for rc in range(0, R, RC):
                rows = pl.ds(rc, RC)
                dp = dot(dr[rows], vb, NT)
                e = Pm[rows, cols].astype(F32)
                dl = mx[rows]
                ds = jnp.concatenate([e[:, k : k + 128] * (dp[:, k : k + 128] - dl) for k in range(0, KB, 128)], axis=1).astype(BF)
                D[rows] = ds
                dqacc[rows] += dot(ds, kb, NN)
            dk = dot(qr[...], D[...], TN).T * INV
            dv = dot(dr[...], Pm[:, cols], TN).T
            return dk, dv

        def step(i, _):
            dkv = block(prefix_rows(h, 0, prompt, i), prefix_rows(h, 1, prompt, i), pl.multiple_of(i * KB, KB))
            for kv in range(2):
                if b == 0:
                    X[kv, i] = dkv[kv]
                else:
                    before = pid[2 * p]
                    for a in range(2):
                        e = jnp.where(before == a, X[kv, i], 0.0) + jnp.where(prompt == a, dkv[kv], 0.0)
                        tm[h, kv, a, i] = e.astype(BF).reshape(4, 4, 64, HD)
            return 0

        lax.fori_loop(0, PRE // KB, step, 0)
        dkv = block(res[0, h, b], res[1, h, b], PRE)
        for kv in range(2):
            tm[h, kv, 2, b] = dkv[kv].astype(BF).reshape(4, 4, 64, HD)
        for rc in range(0, R, RC):
            rows = pl.ds(rc, RC)
            e = dqacc[rows] * INV
            if h == 0:
                dqh[b, rows] = e
            else:
                both = jnp.concatenate([dqh[b, rows].reshape(RC // G, G, HD), e.reshape(RC // G, G, HD)], axis=1)
                dqb[b, pl.ds(rc // G, RC // G)] = both.astype(BF)

    ends = []

    def swap_out(b, s, d):
        ends.append(mv.to(s.at[b, pl.ds(T2 * (1 - m), T2)], d.at[b, :, pl.ds(16 * m, 16)], mate))
        owns.append(mv.here(s.at[b, pl.ds(T2 * m, T2)], d.at[b, :, pl.ds(16 * m, 16)]))

    owns = []

    def pair_sum(h, cp):
        cp.wait_recv()
        for i in range(3):
            for j in range(2):
                for k in range(4):
                    s0[h, i, j, k] = (tm[h, c, i, j, k].astype(F32) + far[h, i, j, k].astype(F32)).astype(BF)
        a = [mv.to(s0.at[h, 0, :, :, (x + 1 + d) % 4], r1.at[h, 0, d], xs[d]) for d in range(3)]
        b = [mv.to(s0.at[h, 1, :, (y + 1 + d) % 4], r1.at[h, 1, d], ys[d]) for d in range(3)]
        e = [mv.to(s0.at[h, 2, :, (x + 1 + d) % 4], rr1.at[h, d], xs[d]) for d in range(3)]
        return a, b, e

    def second(h, cps):
        sent = []
        for a in range(2):
            got(cps[a])
            for j in range(2):
                for k in range(4):
                    t = (s0[h, 0, j, k, x] if a == 0 else s0[h, 1, j, y, k]).astype(F32)
                    for d in range(3):
                        t = t + r1[h, a, d, j, k].astype(F32)
                    s1[h, a, j, k] = t.astype(BF)
            at = y if a == 0 else x
            sent.append([mv.to(s1.at[h, a, :, (at + 1 + d) % 4], r2.at[h, a, d], (ys if a == 0 else xs)[d]) for d in range(3)])
        return sent

    def resp_sum(h, cps):
        got(cps[2])
        for b in range(2):
            for k in range(4):
                t = s0[h, 2, b, x, k].astype(F32)
                for d in range(3):
                    t = t + rr1[h, d, b, k].astype(F32)
                rs[c, h, b, k] = t.astype(BF)
        at = rs.at[c, h, :, pl.ds(2 * (1 - c), 2)]
        return mv.to(at, at, sib)

    def resp_out(h, cp):
        cp.wait_recv()
        owns.append(mv.here(rs.at[:, h, :, 2 * c + m], fr.at[:, 2 * m + h]))
        ends.append(mv.to(rs.at[:, h, :, 2 * c + 1 - m], fr.at[:, 2 * m + h], mate))

    def third(h, cps):
        for a in range(2):
            got(cps[a])
            for j in range(2):
                t = s1[h, a, j, y if a == 0 else x].astype(F32)
                for d in range(3):
                    t = t + r2[h, a, d, j].astype(F32)
                s2[h, a, j] = t.astype(BF)
        return mv.to(s2.at[h, :, 1 - zl], r3.at[h], zmate)

    def final(h, cp):
        cp.wait_recv()
        for a in range(2):
            fin[c, h, a, x] = (s2[h, a, zl].astype(F32) + r3[h, a].astype(F32)).astype(BF)
        at = fin.at[c, h, :, x]
        ends.append(mv.to(at, at, sib))
        return [mv.to(at, at, w) for w in xs]

    def twin(h, cps):
        for d in (0, 2, 1):
            cps[d].wait_recv()
            at = fin.at[c, h, :, (x + 3 - d) % 4]
            ends.append(mv.to(at, at, sib))

    pass_a(0, 0)
    vs += pass_y(vy, vy2, pv_at)
    q_in[1], g_in[1] = swap_in(1, q, qb), swap_in(1, g, gb)
    pz, py = spread_z(pkv.at[:, 1, :, pl.ds(half, 128)], p1_at)
    rx1, rs1 = spread_r(1)
    got([g_in[0]] + vs)
    pass_b(0, 0)
    pass_c(0, 0)
    py2, ps = pass_z(pz, p1_at)
    rs1 += pass_r((rx1, None, lambda xx: r_at(1, xx)))
    for cp in own_q[1]:
        cp.wait()
    got([q_in[1], g_in[1]])
    pass_a(0, 1)
    ps += pass_y(py, py2, p1_at)
    pass_b(0, 1)
    pass_c(0, 1)
    first0 = mv.to(tm.at[0, 1 - c], far.at[0], sib)
    got(ps + rs1)
    pass_a(1, 0)
    a0 = pair_sum(0, first0)
    pass_b(1, 0)
    swap_out(0, ob, out)
    pass_c(1, 0)
    swap_out(0, dqb, dout)
    b0 = second(0, a0)
    e0 = resp_sum(0, a0)
    pass_a(1, 1)
    z0 = third(0, b0)
    resp_out(0, e0)
    pass_b(1, 1)
    swap_out(1, ob, out)
    f0 = final(0, z0)
    pass_c(1, 1)
    first1 = mv.to(tm.at[1, 1 - c], far.at[1], sib)
    swap_out(1, dqb, dout)
    twin(0, f0)
    a1 = pair_sum(1, first1)
    b1 = second(1, a1)
    e1 = resp_sum(1, a1)
    z1 = third(1, b1)
    resp_out(1, e1)
    f1 = final(1, z1)
    twin(1, f1)
    got(ends)
    for cp in owns:
        cp.wait()
    mv.drain()


def fused(pid, plens, rlens, q, g, rkv, pkv):
    v = pltpu.VMEM
    n = 128
    return pl.pallas_call(
        kernel,
        out_shape=[jax.ShapeDtypeStruct((2, T2, 32, HD), BF)] * 2
        + [jax.ShapeDtypeStruct((2, 2, 2, 4, 64, HD), BF), jax.ShapeDtypeStruct((2, 4, 2, 64, HD), BF)],
        in_specs=[SM] * 3 + [HBM] * 4,
        out_specs=[HBM, HBM, VM, VM],
        scratch_shapes=[
            v((2, T, 16, HD), BF), v((2, T, 16, HD), BF),
            v((2, 2, 1024, HD), BF), v((2, 2, 1024, HD), BF), v((2, 2, 2, 1024, HD), BF), v((2, 2, 2, 1024, HD), BF),
            v((R, PRE + RL), F32), v((R, PRE + RL), BF), v((R, KB), BF),
            v((R, 2 * HD), BF), v((R, HD), BF), v((R, HD), BF),
            v((R, 128), F32), v((R, 128), F32), v((R, HD), F32), v((R, HD), F32),
            v((2, 2, 1024, HD), F32), v((2, R, HD), F32), v((2, R, HD), F32), v((2, T, 16, HD), BF), v((2, T, 16, HD), BF),
            v((2, 2, 3, 2, 4, 4, 64, HD), BF), v((2, 3, 2, 4, 4, 64, HD), BF), v((2, 3, 2, 4, 4, 64, HD), BF),
            v((2, 2, 3, 2, 4, 64, HD), BF), v((2, 2, 2, 4, 64, HD), BF),
            v((2, 2, 3, 2, 64, HD), BF), v((2, 2, 2, 64, HD), BF), v((2, 2, 64, HD), BF),
            v((2, 3, 2, 4, 64, HD), BF), v((2, 2, 2, 4, 64, HD), BF),
            pltpu.SemaphoreType.DMA((n,)), pltpu.SemaphoreType.DMA((n,)), pltpu.SemaphoreType.DMA((32,)),
        ],
        compiler_params=pltpu.CompilerParams(collective_id=1, has_side_effects=True, vmem_limit_bytes=62 * 2**20),
    )(pid, plens, rlens, q, g, rkv, pkv)


def per_device(queries, resp_keys, resp_values, prefix_keys, prefix_values, grad_out, prompt_ids, prefix_lengths, resp_lengths):
    rkv = jnp.stack([resp_keys, resp_values]).transpose(0, 3, 1, 2, 4)
    pkv = jnp.stack([prefix_keys, prefix_values]).transpose(0, 3, 1, 2, 4)
    attention, d_queries, fin, fr = fused(prompt_ids, prefix_lengths, resp_lengths, queries, grad_out, rkv, pkv)
    fin = fin.reshape(2, 2, 2, 256, HD).transpose(0, 2, 3, 1, 4)
    fr = fr.transpose(0, 2, 3, 1, 4)
    return (attention, d_queries, fr[0], fr[1], fin[0], fin[1])


def solution(mesh):
    rows = P("prefix", ("resp", "mp"), None, None)
    pre = P(None, "prefix", "mp", None)
    return jax.shard_map(
        per_device,
        mesh=mesh,
        in_specs=(rows, rows, rows, pre, pre, rows, P(), P(), P()),
        out_specs=(rows, rows, rows, rows, pre, pre),
        check_vma=False,
    )
```

time: 347 us -> 132 us (0.38)
  waiting for transfers between devices: 153 us -> 0 us
  Pallas kernels: 51.4 us -> 121 us
  starting transfers between devices: 52.3 us -> 0 us
  blocking collectives: 26.6 us -> 0 us
  local copies, waits for them, and re-layouts: 32.8 us -> 8.3 us
  other arithmetic: 16.3 us -> 1.57 us
  between operations: 14.2 us -> 0.69 us
    all_to_all x7 -> x0, waiting for transfers between devices: 153 us -> none  [the longest x1 49.2 us: per_device(): q = lax.all_to_all(queries, 'mp', split_axis=2, concat_axis=1, tiled=True)]
    pallas_call x1, Pallas kernels: 51.4 us -> 121 us  [fused(): pl.pallas_call(kernel, out_shape=[jax.ShapeDtypeStruct((2, T2, 32, HD), B...]
    all_to_all x7 -> x0, starting transfers between devices: 52.2 us -> none  [the longest x1 21.2 us: per_device(): lax.all_to_all(pt, ('prefix', 'resp'), split_axis=3, concat_axis=3, tiled...]
    all_gather x1 -> x0, blocking collectives: 15.5 us -> none  [per_device(): pt = lax.all_gather(pt, 'resp', axis=3, tiled=True).transpose(0, 2, 3, 1, 4)]
    all_to_all x1 -> x0, blocking collectives: 11 us -> none  [per_device(): kv = lax.all_to_all(kv, 'mp', split_axis=3, concat_axis=2, tiled=True)]
    all_to_all x6 -> x0, local copies, waits for them, and re-layouts: 8.8 us -> none  [the longest x1 2.37 us: per_device(): attention = lax.all_to_all(o, 'mp', split_axis=1, concat_axis=2, tiled=True)]
    reduce_sum x2 -> x0, other arithmetic: 4.99 us -> none  [the longest x1 3.02 us: per_device(): pt = jnp.sum(pt.astype(jnp.float32), axis=3).astype(jnp.bfloat16)]
    pallas_call x2 -> x0, local copies, waits for them, and re-layouts: 4.9 us -> none  [per_device(): o, dq, dk, dv = attend()(meta, q, c, flat[0], flat[1])]
  transfers between devices with their start and end apart: 9 -> 0, of which waited for: 6 -> 0; matrix products, arithmetic and copies ran while one was open for 10% -> 0% of each run, Pallas kernels for 0% -> 0%
where the time goes in v3:
time: 132 us
  Pallas kernels  121 us (92%)
  local copies, waits for them, and re-layouts  8.3 us (6%)
  other arithmetic  1.57 us (1%)
    pallas_call x1, Pallas kernels, fused(): pl.pallas_call(kernel, out_shape=[jax.ShapeDtypeStruct((2, T2, 32, HD), B...  121 us
    unnamed x14, local copies, waits for them, and re-layouts  4.48 us

profile of v3, /device:TPU:1, one launch (start us, length us, event | category | flops | bytes accessed | tf_op | source)
XLA Modules:
  0.0 131.6 jit_solution(936650336156847373)
XLA Ops:
  0.6 1.0 copy_bitcast_fusion.3
  1.6 0.0 copy-start.3
  1.7 0.0 copy-start.4
  1.7 0.7 maximum_bitcast_fusion.1.rkv
  2.4 0.2 copy-done.3
  2.7 0.1 copy-done.4
  2.8 0.1 copy_bitcast_fusion.1
  2.9 0.8 maximum_bitcast_fusion.pkv
  3.7 121.0 %shard_map.136 = (bf16[2,64,32,128]{3,2,1,0:T(8,128)(2,1)}, bf16[2,64,32,128]{3,2,1,0:T(8,128)(2,1)}, bf16[2,2,2,4,64,128]{5,4,3,2,1,0:T(8,128)(2,1)}, bf16[2,4,2,64,128]{4,3,2,1,0:T(8,128)(2,1)}) custom-call(s32[16]{0:T(128)} %pid.1, s32[2]{0:T(128)} %plen_ref.1, s32[16]{0:T(128)} %rlen_ref.1, bf16[2,64,32,128]{3,2,1,0:T(8,128)(2,1)} %q.1, ...), custom_call_target="tpu_custom_call" | custom-call | tf_op jit(solution)/shard_map/pallas_call | solution.py:408
  124.7 0.0 copy-start.2
  124.7 1.0 slice_bitcast_fusion.2
  125.8 0.8 copy.21
  126.5 0.8 copy.20
  127.3 0.0 copy-done.2
  127.3 0.0 copy-start.1
  127.3 0.5 copy.27
  127.9 1.2 slice_bitcast_fusion
  129.0 0.0 copy-done.1
  129.0 0.0 copy-start
  129.0 1.0 copy.30
  130.0 0.6 copy-done
  130.6 1.0 copy.31
Async XLA Ops:
  1.6 1.0 copy-start.3
  1.7 1.1 copy-start.4
  124.7 2.6 %copy-start.2 = (bf16[2,2,2,4,64,128]{5,4,3,2,1,0:T(8,128)(2,1)S(1)}, bf16[2,2,2,4,64,128]{5,4,3,2,1,0:T(8,128)(2,1)}, u32[]{:S(2)}) copy-start(bf16[2,2,2,4,64,128]{5,4,3,2,1,0:T(8,128)(2,1)} %get-tuple-element.13) | copy-start | bytes 1572868
  127.3 1.7 %copy-start.1 = (bf16[2,64,32,128]{3,2,1,0:T(8,128)(2,1)S(1)}, bf16[2,64,32,128]{3,2,1,0:T(8,128)(2,1)}, u32[]{:S(2)}) copy-start(bf16[2,64,32,128]{3,2,1,0:T(8,128)(2,1)} %get-tuple-element.34) | copy-start | bytes 3145732
  129.0 1.6 %copy-start = (bf16[2,64,32,128]{3,2,1,0:T(8,128)(2,1)S(1)}, bf16[2,64,32,128]{3,2,1,0:T(8,128)(2,1)}, u32[]{:S(2)}) copy-start(bf16[2,64,32,128]{3,2,1,0:T(8,128)(2,1)} %get-tuple-element.35) | copy-start | bytes 3145732
